TPU v7x, 256 devices: a whole 4x4x8 slice. The times are simulated.
256 devices in a mesh: long: 16 (over y, x_hi, core), inner: 16 (over x_lo, z).
Axes of the slice: x: 4 (x_hi: 2, x_lo: 2; x = x_hi * 2 + x_lo), y: 4, z: 8, core: 2. Of those that a mesh axis runs over, the one named last changes fastest.
Arguments:
- image_raw: bfloat16 [16384, 1280], P(('long', 'inner')), may hold values from -1 to 1, as said below
- text_raw: bfloat16 [16384, 1280], P(('long', 'inner')), may hold values from -1 to 1, as said below
- log_scale: float32 [1], replicated, may hold values from 4 to 4.6
Outputs:
- grad_image: bfloat16 [16384, 1280], P(('long', 'inner'))
- grad_text: bfloat16 [16384, 1280], P(('long', 'inner'))
- loss: float32 [1], replicated
- grad_log_scale: float32 [1], replicated
Inputs may be any that keep to these rules, and one draw needn't show every extreme that they name: `image_raw`: each image row and its paired text row are partly aligned. `text_raw`: each text row and its paired image row are partly aligned.
All inputs are finite; a program needn't handle non-finite values.
Results may differ from a plain program's by a relative error of at most 0.017.
Values may be sent and summed in bfloat16 or wider, within the bound.
No kernel may reach another device: no remote copies, remote signals or barrier semaphores. Data moves between devices by JAX's collectives and lax.ppermute only.
A program may use at most 64 MiB of HBM per device.

v0:
```python
import itertools

import jax
import jax.numpy as jnp
from jax import lax
from jax.experimental import pallas as pl
from jax.experimental.pallas import tpu as pltpu
from jax.sharding import Mesh, PartitionSpec as P

NORM_EPS = 1e-06
AXES = ("y", "xh", "c", "xl", "z")
SIZES = (4, 2, 2, 2, 8)
GROUP = 16
ROWS = 64
VMEM_LIMIT = 24 * 1024 * 1024
F32 = jnp.float32
BF16 = jnp.bfloat16
VMEM = pl.BlockSpec(memory_space=pltpu.VMEM)
SMEM = pl.BlockSpec(memory_space=pltpu.SMEM)


def call(kernel, out, ins, name, flops=0, **more):
    return pl.pallas_call(
        kernel,
        out_shape=out,
        in_specs=ins,
        compiler_params=pltpu.CompilerParams(vmem_limit_bytes=VMEM_LIMIT),
        cost_estimate=pl.CostEstimate(flops=flops, bytes_accessed=1 << 20, transcendentals=0),
        name=name,
        **more,
    )


def shape(*dims, dtype=BF16):
    return jax.ShapeDtypeStruct(dims, dtype)


def permute(array, move):
    flat = lambda x, y, z, c: (((y * 2 + x // 2) * 2 + c) * 2 + x % 2) * 8 + z
    pairs = []
    for y, xh, c, xl, z in itertools.product(*map(range, SIZES)):
        x2, y2, z2, c2 = move(2 * xh + xl, y, z, c)
        pairs.append((flat(2 * xh + xl, y, z, c), flat(x2 % 4, y2 % 4, z2 % 8, c2 % 2)))
    return lax.ppermute(array, AXES, pairs)


def to_sibling(array):
    return permute(array, lambda x, y, z, c: (x, y, z, 1 - c))


def along(array, axis, step):
    steps = {"x": (step, 0, 0), "y": (0, step, 0), "z": (0, 0, step)}[axis]
    return permute(array, lambda x, y, z, c: (x + steps[0], y + steps[1], z + steps[2], c))


def first_axis(array, step):
    return permute(array, lambda x, y, z, c: (x + step, y, z, c) if c == 0 else (x, y + step, z, c))


def second_axis(array, step):
    return permute(array, lambda x, y, z, c: (x, y + step, z, c) if c == 0 else (x + step, y, z, c))


def ring(array, step):
    return permute(array, lambda x, y, z, c: (x, y, z + (step if c == 0 else -step), c))


def normalize_kernel(img_ref, txt_ref, img_hat_ref, txt_hat_ref, diag_ref):
    hats = []
    for raw, hat in ((img_ref, img_hat_ref), (txt_ref, txt_hat_ref)):
        values = raw[...].astype(F32)
        recip = 1.0 / jnp.sqrt(jnp.sum(values * values, axis=1, keepdims=True) + NORM_EPS)
        hat[...] = (values * recip).astype(BF16)
        hats.append(hat[...].astype(F32))
    diag_ref[...] = jnp.full(diag_ref.shape, jnp.sum(hats[0] * hats[1]), F32)


def encode(ref, at, scalars):
    high = scalars.astype(BF16).astype(F32)
    middle = (scalars - high).astype(BF16).astype(F32)
    parts = (high, middle, scalars - high - middle)
    row = lax.broadcasted_iota(jnp.int32, (16, 128), 0)
    block = jnp.zeros((16, 128), F32)
    for k, part in enumerate(parts):
        block = jnp.where(row == k, jnp.concatenate([part, part], axis=0), block)
    ref[at : at + 16, 0:128] = block.astype(BF16)
    ref[at : at + 16, 128:] = jnp.zeros((16, ref.shape[1] - 128), BF16)


def decode(ref, at):
    block = ref[at : at + 16, 0:128].astype(F32)
    return jnp.broadcast_to(jnp.sum(block, axis=0, keepdims=True), (8, 128))


def pair_kernel(core_ref, keep_ref, arrived_ref, far_ref, rest_ref, own_ref, scalar_ref):
    total = keep_ref[0:512, :].astype(F32) + arrived_ref[0:512, :].astype(F32)
    total = total.astype(BF16)
    rest_ref[...] = total[0:384]
    far_ref[0:64, :] = total[384:448]
    own_ref[...] = total[448:512]
    scalars = decode(keep_ref, 512) + decode(arrived_ref, 512)
    scalar_ref[...] = scalars
    encode(far_ref, 64, jnp.where(core_ref[0] == 0, scalars, 0.0))


def ring_fold_kernel(start, base_ref, arrived_ref, scalar_ref, out_ref):
    rows = arrived_ref.shape[0] - 16
    out_ref[0:rows, :] = (
        base_ref[start : start + rows, :].astype(F32) + arrived_ref[0:rows, :].astype(F32)
    ).astype(BF16)
    if rows < 128:
        out_ref[rows:128, :] = base_ref[start + rows : start + 128, :]
    encode(out_ref, 128, scalar_ref[...] + decode(arrived_ref, rows))


def plane_fold_kernel(minus_ref, plus_ref, low_ref, high_ref, scalar_ref, to_minus_ref, to_plus_ref):
    to_minus_ref[0:128, :] = (minus_ref[0:128, :].astype(F32) + low_ref[0:128, :].astype(F32)).astype(BF16)
    to_minus_ref[128:256, :] = minus_ref[128:256, :]
    to_plus_ref[0:128, :] = plus_ref[0:128, :]
    to_plus_ref[128:256, :] = (plus_ref[128:256, :].astype(F32) + high_ref[...].astype(F32)).astype(BF16)
    encode(to_minus_ref, 256, scalar_ref[...] + decode(low_ref, 128))
    encode(to_plus_ref, 256, scalar_ref[...])


def line_kernel(own_ref, down_ref, up_ref, scalar_ref, *outs):
    scalars = scalar_ref[...] + decode(down_ref, 256) + decode(up_ref, 256)
    for k, out in enumerate(outs[:4]):
        cut = slice(k * 64, (k + 1) * 64)
        out[0:64, :] = (
            own_ref[cut, :].astype(F32) + down_ref[cut, :].astype(F32) + up_ref[cut, :].astype(F32)
        ).astype(BF16)
        if k:
            encode(out, 64, scalars)
    outs[4][...] = scalars


def logits_kernel(counts, *refs):
    row_place, col_place, scale_ref, diag_ref = refs[:4]
    n_img, n_txt = len(counts[0]), len(counts[1])
    img_refs, txt_refs = refs[4 : 4 + n_img], refs[4 + n_img : 4 + n_img + n_txt]
    img_all, txt_all, logit_ref, row_ref, col_ref, row_acc = refs[4 + n_img + n_txt :]
    step = pl.program_id(0)
    tile = 256

    @pl.when(step == 0)
    def _():
        for blocks, sizes, target in ((img_refs, counts[0], img_all), (txt_refs, counts[1], txt_all)):
            at = 0
            for block, size in zip(blocks, sizes):
                target[at : at + size, :] = block[...]
                at += size
        row_acc[...] = jnp.zeros_like(row_acc)

    start = pl.multiple_of(step * tile, tile)
    block = txt_all[pl.ds(start, tile), :]
    logits = scale_ref[0] * lax.dot_general(
        img_all[...], block, (((1,), (1,)), ((), ())), preferred_element_type=F32
    )
    logit_ref[:, pl.ds(start, tile)] = logits
    powers = jnp.exp(logits - scale_ref[1])
    weighted = powers * logits
    for k in range(tile // 128):
        row_acc[0] += powers[:, k * 128 : (k + 1) * 128]
        row_acc[1] += weighted[:, k * 128 : (k + 1) * 128]
    sums = jnp.sum(powers, axis=0, keepdims=True)
    slopes = jnp.sum(weighted, axis=0, keepdims=True)
    for k in range(tile // 64):
        at = col_place[step * (tile // 64) + k]
        cut = slice(k * 64, (k + 1) * 64)
        col_ref[pl.ds(at, 1), :] = jnp.concatenate([sums[:, cut], slopes[:, cut]], axis=1)

    @pl.when(step == pl.num_programs(0) - 1)
    def _():
        sums = jnp.sum(row_acc[0].T, axis=0, keepdims=True)
        slopes = jnp.sum(row_acc[1].T, axis=0, keepdims=True)
        for k in range(GROUP):
            cut = slice(k * 64, (k + 1) * 64)
            row_ref[pl.ds(row_place[k], 1), :] = jnp.concatenate([sums[:, cut], slopes[:, cut]], axis=1)
        row_ref[16:24, :] = diag_ref[...]


def grad_img_kernel(half, *refs):
    row_place, col_place, scale_ref, logit_ref, txt_ref = refs[:5]
    rows_in, cols_in = refs[5:8], refs[8:12]
    grad_ref, dlogit_ref, *row_scalars = refs[12:-4]
    row_sum, col_sum, row_half, col_half = refs[-4:]
    step = pl.program_id(0)
    tile = 256

    @pl.when(step == 0)
    def _():
        row_sum[...] = rows_in[0][...] + rows_in[1][...] + rows_in[2][...]
        col_sum[...] = cols_in[0][...] + cols_in[1][...] + cols_in[2][...] + cols_in[3][...]
        row = jnp.concatenate([row_sum[pl.ds(row_place[half * 8 + k], 1), 0:64] for k in range(8)], axis=1)
        col = jnp.concatenate([col_sum[pl.ds(col_place[k], 1), 0:64] for k in range(16)], axis=1)
        row_half[...] = jnp.broadcast_to(0.5 / row, (128, 512)).T
        col_half[...] = 0.5 / col
        lane = lax.broadcasted_iota(jnp.int32, (8, 128), 1)

        def scalars(sums, last):
            log_sum = jnp.sum(jnp.log(sums[0:16, 0:64]))
            slope = 0.5 * jnp.sum(sums[0:16, 64:128] / sums[0:16, 0:64])
            return jnp.where(lane == 0, log_sum, jnp.where(lane == 1, slope, last))

        encode(grad_ref, 512, scalars(col_sum, 0.0))
        for out in row_scalars:
            out[...] = scalars(row_sum, row_sum[16:24, :])

    start = pl.multiple_of(step * tile, tile)
    powers = jnp.exp(logit_ref[pl.ds(half * 512 + start, tile), :] - scale_ref[1])
    by_row = jnp.concatenate([row_half[pl.ds(start, tile), :]] * 8, axis=1)
    dlogit = (powers * (by_row + col_half[...])).astype(BF16)
    dlogit_ref[pl.ds(start, tile), :] = dlogit
    grad_ref[pl.ds(start, tile), :] = jnp.dot(dlogit, txt_ref[...], preferred_element_type=F32).astype(BF16)


def grad_txt_kernel(low_ref, high_ref, img_ref, scalar_ref, *outs):
    step = pl.program_id(0)
    tile = 256
    start = pl.multiple_of(step * tile, tile)
    grad = sum(
        lax.dot_general(
            part[:, pl.ds(start, tile)],
            img_ref[k * 512 : (k + 1) * 512, :],
            (((0,), (0,)), ((), ())),
            preferred_element_type=F32,
        )
        for k, part in enumerate((low_ref, high_ref))
    ).astype(BF16)
    for k, ref in enumerate(outs[:3]):

        @pl.when(step == k)
        def _():
            ref[...] = grad

    @pl.when(step == 3)
    def _():
        outs[3][0:128, :] = grad[0:128]
        outs[4][...] = grad[128:256]
        encode(outs[3], 128, scalar_ref[...])


def finish_kernel(scale_ref, img_ref, txt_ref, img_hat_ref, txt_hat_ref, *refs):
    own_img, ring_img, sib_img, own_txt, txt1, txt2, txt3, col_ref, row_ref = refs[:9]
    grad_img_ref, grad_txt_ref, loss_ref, slope_ref = refs[9:]
    scale = scale_ref[0]
    for raw, other, parts, out in (
        (img_ref, txt_hat_ref, (own_img, ring_img, sib_img), grad_img_ref),
        (txt_ref, img_hat_ref, (own_txt, txt1, txt2, txt3), grad_txt_ref),
    ):
        values = raw[...].astype(F32)
        recip = 1.0 / jnp.sqrt(jnp.sum(values * values, axis=1, keepdims=True) + NORM_EPS)
        unit = values * recip
        total = sum(part[0:64, :].astype(F32) for part in parts)
        grad_hat = scale * (total - other[...].astype(F32))
        inner = jnp.sum(grad_hat * unit, axis=1, keepdims=True)
        out[...] = (recip * (grad_hat - unit * inner)).astype(BF16)
    cols = col_ref[...] + decode(ring_img, 128) + decode(sib_img, 64)
    rows = row_ref[...] + decode(txt1, 64) + decode(txt2, 64) + decode(txt3, 64)
    batch = ROWS * GROUP * GROUP
    diag_sum = scale * rows[0, 2]
    logs = cols[0, 0] + rows[0, 0] + 2.0 * batch * scale_ref[1]
    loss_ref[0] = (logs - 2.0 * diag_sum) / (2 * batch)
    slope_ref[0] = (cols[0, 1] + rows[0, 1] - diag_sum) / batch


def places():
    y, z, core = lax.axis_index("y"), lax.axis_index("z"), lax.axis_index("c")
    x = 2 * lax.axis_index("xh") + lax.axis_index("xl")
    near = jnp.array([0, 3, 1, 2], jnp.int32)
    first, second = jnp.tile(near, 4), jnp.repeat(near, 4)
    on_x = jnp.where(core == 0, first, second)
    on_y = jnp.where(core == 0, second, first)
    cols = ((y + on_y) % 4) * 4 + (x + on_x) % 4
    distance = jnp.array([-1, -1, -2, -2, -3, -3, -4, 0, 1, 1, 2, 2, 3, 3, 4, 0], jnp.int32)
    others = jnp.array([1, 0, 1, 0, 1, 0, 1, 1, 0, 1, 0, 1, 0, 1, 0, 0], jnp.int32)
    way = jnp.where(core == 0, -1, 1)
    rows = ((core + others) % 2) * 8 + (z + way * distance) % 8
    return rows.astype(jnp.int32), cols.astype(jnp.int32)


def per_device(image_raw, text_raw, log_scale):
    rows, width = image_raw.shape
    total = rows * GROUP
    img_hat, txt_hat, diag = call(
        normalize_kernel,
        (shape(rows, width), shape(rows, width), shape(8, 128, dtype=F32)),
        [VMEM] * 2,
        "normalize",
    )(image_raw, text_raw)

    scale = jnp.exp(log_scale[0])
    shift = jnp.maximum(1.01 * scale - 70.0, 0.0)
    scales = jnp.stack([scale, shift])
    row_place, col_place = places()

    below, above, far = first_axis(txt_hat, 1), first_axis(txt_hat, -1), first_axis(txt_hat, 2)
    sib = to_sibling(img_hat)
    chip = jnp.concatenate([img_hat, sib], axis=0)
    ring1 = ring(chip, 1)
    line = jnp.concatenate([txt_hat, below, above, far], axis=0)
    ring1, line = lax.optimization_barrier((ring1, line))
    up, down = second_axis(line, 1), second_axis(line, -1)
    ring2 = ring(ring1, 1)
    low_far, high_far = second_axis(up[:128], 1), second_axis(down[128:], -1)
    ring3 = ring(ring2, 1)
    ring4 = ring(ring3[:64], 1)
    mine = [ring1, ring2, ring3, ring4]
    img_blocks = [to_sibling(block) for block in mine] + [sib] + mine + [img_hat]
    txt_blocks = [line, up, down, low_far, high_far]
    counts = [[block.shape[0] for block in blocks] for blocks in (img_blocks, txt_blocks)]

    steps = total // 256
    flops = 2 * total * total * width
    img_all, txt_all, logits, row_part, col_part = call(
        lambda *refs: logits_kernel(counts, *refs),
        (
            shape(total, width),
            shape(total, width),
            shape(total, total, dtype=F32),
            shape(24, 128, dtype=F32),
            shape(16, 128, dtype=F32),
        ),
        [SMEM] * 3 + [VMEM] * (1 + len(img_blocks) + len(txt_blocks)),
        "logits",
        flops,
        grid=(steps,),
        out_specs=(VMEM,) * 5,
        scratch_shapes=[pltpu.VMEM((2, total, 128), F32)],
    )(row_place, col_place, scales, diag, *img_blocks, *txt_blocks)

    row_pair = row_part + to_sibling(row_part)
    col_line = col_part + along(col_part, "x", 1) + along(col_part, "x", 2) + along(col_part, "x", 3)
    lower, upper = along(row_pair, "z", 1), along(row_pair, "z", -1)
    two = row_pair + lower
    three = two + upper
    row_parts = [three, along(three, "z", 3), along(two, "z", -3)]
    col_parts = [col_line] + [along(col_line, "y", k) for k in (1, 2, 3)]

    def grad_img(half):
        row_scalars = (shape(8, 128, dtype=F32),) if half == 0 else ()
        return call(
            lambda *refs: grad_img_kernel(half, *refs),
            (shape(total // 2 + 16, width), shape(total // 2, total)) + row_scalars,
            [SMEM] * 3 + [VMEM] * 9,
            f"grad_img{half}",
            flops // 2,
            grid=(steps // 2,),
            out_specs=(VMEM,) * (2 + len(row_scalars)),
            scratch_shapes=[
                pltpu.VMEM((24, 128), F32),
                pltpu.VMEM((16, 128), F32),
                pltpu.VMEM((total // 2, 128), F32),
                pltpu.VMEM((1, total), F32),
            ],
        )(row_place, col_place, scales, logits, txt_all, *row_parts, *col_parts)

    core = jnp.reshape(lax.axis_index("c"), (1,)).astype(jnp.int32)
    send, dlogits_low, row_scalars = grad_img(0)
    arrived = to_sibling(send)
    keep, dlogits_high = grad_img(1)
    far, rest, own_img, col_scalars = call(
        pair_kernel,
        (shape(80, width), shape(384, width), shape(64, width), shape(8, 128, dtype=F32)),
        [SMEM] + [VMEM] * 2,
        "pair",
    )(core, keep, arrived)
    ring1 = ring(far, -1)
    txt_own, txt_minus, txt_plus, far_low, far_high = call(
        grad_txt_kernel,
        (shape(256, width),) * 3 + (shape(144, width), shape(128, width)),
        [VMEM] * 4,
        "grad_txt",
        flops,
        grid=(steps,),
        out_specs=(VMEM,) * 5,
    )(dlogits_low, dlogits_high, img_all, row_scalars)

    def ring_fold(start, arrived):
        return call(
            lambda *refs: ring_fold_kernel(start, *refs), shape(144, width), [VMEM] * 3, "ring_fold"
        )(rest, arrived, col_scalars)

    ring1, far_low, far_high = lax.optimization_barrier((ring1, far_low, far_high))
    low, high = second_axis(far_low, -1), second_axis(far_high, 1)
    ring2 = ring(ring_fold(256, ring1), -1)
    ring2, low, high = lax.optimization_barrier((ring2, low, high))
    to_minus, to_plus = call(
        plane_fold_kernel, (shape(272, width),) * 2, [VMEM] * 5, "plane_fold"
    )(txt_minus, txt_plus, low, high, row_scalars)
    down, up = second_axis(to_minus, -1), second_axis(to_plus, 1)
    ring3 = ring(ring_fold(128, ring2), -1)
    ring3, down, up = lax.optimization_barrier((ring3, down, up))
    own_txt, *sends, row_scalars = call(
        line_kernel,
        (shape(64, width),) + (shape(80, width),) * 3 + (shape(8, 128, dtype=F32),),
        [VMEM] * 4,
        "line",
    )(txt_own, down, up, row_scalars)
    ring4 = ring(ring_fold(0, ring3), -1)
    txt_parts = [own_txt] + [first_axis(part, step) for part, step in zip(sends, (-1, 1, 2))]
    img_parts = [own_img, ring4, to_sibling(ring4[64:])]

    scalar = shape(1, dtype=F32)
    return call(
        finish_kernel,
        (shape(rows, width), shape(rows, width), scalar, scalar),
        [SMEM] + [VMEM] * 13,
        "finish",
        out_specs=(VMEM, VMEM, SMEM, SMEM),
    )(scales, image_raw, text_raw, img_hat, txt_hat, *img_parts, *txt_parts, col_scalars, row_scalars)


def solution(mesh):
    mesh = Mesh(mesh.devices.reshape(SIZES), AXES)
    spec = P(AXES, None)
    return jax.shard_map(
        per_device, mesh=mesh, in_specs=(spec, spec, P()), out_specs=(spec, spec, P(), P()), check_vma=False
    )
```

profile of v0, /device:TPU:160, one launch (start us, length us, event | category | flops | bytes accessed | tf_op | source)
XLA Modules:
  0.0 130.6 jit_solution(17384916839291640395)
XLA Ops:
  0.7 0.9 copy-done
  1.6 0.9 copy-done.2
  2.5 0.4 normalize.1
  2.9 0.1 collective-permute-start
  3.0 3.1 %collective-permute-start.4 = (bf16[64,1280]{1,0:T(8,128)(2,1)S(1)}, bf16[64,1280]{1,0:T(8,128)(2,1)S(1)}, u32[]{:S(2)}, u32[]{:S(2)}) collective-permute-start(bf16[64,1280]{1,0:T(8,128)(2,1)S(1)} %get-tuple-element.45.txt_hat_ref), channel_id=1, source_target_pairs={{0,32},{1,33},{2,34},{3,35},{4,36},{5,37},{6,38},{7,39},{8,40},{9,... | collective-permute-start | bytes 491528 | tf_op jit(solution)/shard_map/ppermute | solution.py:44
  6.1 1.1 collective-permute-start.3
  7.2 0.9 collective-permute-start.2
  8.2 1.1 collective-permute-start.1
  9.3 0.6 collective-permute-done.4
  9.9 1.8 %collective-permute-done.3 = bf16[64,1280]{1,0:T(8,128)(2,1)S(1)} collective-permute-done((bf16[64,1280]{1,0:T(8,128)(2,1)S(1)}, bf16[64,1280]{1,0:T(8,128)(2,1)S(1)}, u32[]{:S(2)}, u32[]{:S(2)}) %collective-permute-start.3) | collective-permute-done | bytes 163872 | tf_op jit(solution)/shard_map/ppermute | solution.py:44
  11.7 2.0 %collective-permute-done.2 = bf16[64,1280]{1,0:T(8,128)(2,1)S(1)} collective-permute-done((bf16[64,1280]{1,0:T(8,128)(2,1)S(1)}, bf16[64,1280]{1,0:T(8,128)(2,1)S(1)}, u32[]{:S(2)}, u32[]{:S(2)}) %collective-permute-start.2) | collective-permute-done | bytes 163872 | tf_op jit(solution)/shard_map/ppermute | solution.py:44
  13.8 1.5 %collective-permute-done.1.refs_9_ = bf16[128,1280]{1,0:T(8,128)(2,1)S(1)} collective-permute-done((bf16[128,1280]{1,0:T(8,128)(2,1)S(1)}, bf16[128,1280]{1,0:T(8,128)(2,1)S(1)}, u32[]{:S(2)}, u32[]{:S(2)}) %collective-permute-start.1) | collective-permute-done | bytes 327712 | tf_op jit(solution)/shard_map/ppermute | solution.py:44
  15.3 1.0 collective-permute-start.6
  16.3 3.0 %collective-permute-start.13 = (bf16[256,1280]{1,0:T(8,128)(2,1)S(1)}, bf16[256,1280]{1,0:T(8,128)(2,1)S(1)}, u32[]{:S(2)}, u32[]{:S(2)}) collective-permute-start(bf16[256,1280]{1,0:T(8,128)(2,1)S(1)} %pad_maximum_fusion.refs_14_), channel_id=1, source_target_pairs={{0,192},{1,193},{2,194},{3,195},{4,196},{5,197},{6,198},{7,199},{8... | collective-permute-start | bytes 1966088 | tf_op jit(solution)/shard_map/ppermute | solution.py:44
  19.3 3.2 %collective-permute-done.6.refs_10_ = bf16[128,1280]{1,0:T(8,128)(2,1)S(1)} collective-permute-done((bf16[128,1280]{1,0:T(8,128)(2,1)S(1)}, bf16[128,1280]{1,0:T(8,128)(2,1)S(1)}, u32[]{:S(2)}, u32[]{:S(2)}) %collective-permute-start.6) | collective-permute-done | bytes 327712 | tf_op jit(solution)/shard_map/ppermute | solution.py:44
  22.6 0.8 collective-permute-start.8
  23.4 7.5 %collective-permute-done.8.refs_11_ = bf16[128,1280]{1,0:T(8,128)(2,1)S(1)} collective-permute-done((bf16[128,1280]{1,0:T(8,128)(2,1)S(1)}, bf16[128,1280]{1,0:T(8,128)(2,1)S(1)}, u32[]{:S(2)}, u32[]{:S(2)}) %collective-permute-start.8) | collective-permute-done | bytes 327712 | tf_op jit(solution)/shard_map/ppermute | solution.py:44
  30.9 0.7 slice.16
  31.8 0.5 collective-permute-start.9
  32.4 3.1 %collective-permute-start.15 = (bf16[128,1280]{1,0:T(8,128)(2,1)S(1)}, bf16[128,1280]{1,0:T(8,128)(2,1)S(1)}, u32[]{:S(2)}, u32[]{:S(2)}) collective-permute-start(bf16[128,1280]{1,0:T(8,128)(2,1)S(1)} %slice.18), channel_id=1, source_target_pairs={{0,192},{1,193},{2,194},{3,195},{4,196},{5,197},{6,198},{7,199},{8... | collective-permute-start | bytes 983048 | tf_op jit(solution)/shard_map/ppermute | solution.py:44
  35.6 2.8 %collective-permute-done.10.refs_12_ = bf16[64,1280]{1,0:T(8,128)(2,1)} collective-permute-done((bf16[64,1280]{1,0:T(8,128)(2,1)}, bf16[64,1280]{1,0:T(8,128)(2,1)}, u32[]{:S(2)}, u32[]{:S(2)}) %collective-permute-start.10) | collective-permute-done | bytes 163872 | tf_op jit(solution)/shard_map/ppermute | solution.py:44
  39.2 0.8 collective-permute-done.11.refs_7_
  40.0 3.8 %collective-permute-done.14.refs_17_ = bf16[128,1280]{1,0:T(8,128)(2,1)S(1)} collective-permute-done((bf16[128,1280]{1,0:T(8,128)(2,1)S(1)}, bf16[128,1280]{1,0:T(8,128)(2,1)S(1)}, u32[]{:S(2)}, u32[]{:S(2)}) %collective-permute-start.14) | collective-permute-done | bytes 327712 | tf_op jit(solution)/shard_map/ppermute | solution.py:44
  43.9 6.1 %logits.1 = (bf16[1024,1280]{1,0:T(8,128)(2,1)S(1)}, bf16[1024,1280]{1,0:T(8,128)(2,1)S(1)}, f32[1024,1024]{1,0:T(8,128)S(1)}, f32[24,128]{1,0:T(8,128)S(1)}, f32[16,128]{1,0:T(8,128)S(1)}) custom-call(s32[16]{0:T(128)S(1)} %get-tuple-element.88.refs_0_, s32[16]{0:T(128)S(1)} %get-tuple-element.89.refs_1_, f32[2]{0:T(128)S(1)} %pad_maximum_fusion.2.refs_2_.scale_ref, ...), custom_call_target="tpu_custom_call" | custom-call | flops 2684354560 | bytes 1048576 | tf_op jit(solution)/shard_map/logits/pallas_call | solution.py:315
  50.0 1.2 collective-permute-done.16
  51.2 3.2 %collective-permute-start.18 = (f32[24,128]{1,0:T(8,128)S(1)}, f32[24,128]{1,0:T(8,128)S(1)}, u32[]{:S(2)}, u32[]{:S(2)}) collective-permute-start(f32[24,128]{1,0:T(8,128)S(1)} %add.94), channel_id=1, source_target_pairs={{0,7},{1,0},{2,1},{3,2},{4,3},{5,4},{6,5},{7,6},{8,15},{9,8},{10,9... | collective-permute-start | bytes 36872 | tf_op jit(solution)/shard_map/ppermute | solution.py:44
  54.4 2.4 %collective-permute-start.23 = (f32[16,128]{1,0:T(8,128)S(1)}, f32[16,128]{1,0:T(8,128)S(1)}, u32[]{:S(2)}, u32[]{:S(2)}) collective-permute-start(f32[16,128]{1,0:T(8,128)S(1)} %get-tuple-element.52), channel_id=1, source_target_pairs={{0,40},{1,41},{2,42},{3,43},{4,44},{5,45},{6,46},{7,47},{8,0},{9,1... | collective-permute-start | bytes 24584 | tf_op jit(solution)/shard_map/ppermute | solution.py:44
  56.8 0.3 collective-permute-start.22
  57.1 0.6 collective-permute-start.21
  57.7 1.7 %collective-permute-done.17 = f32[24,128]{1,0:T(8,128)S(1)} collective-permute-done((f32[24,128]{1,0:T(8,128)S(1)}, f32[24,128]{1,0:T(8,128)S(1)}, u32[]{:S(2)}, u32[]{:S(2)}) %collective-permute-start.17) | collective-permute-done | bytes 12320 | tf_op jit(solution)/shard_map/ppermute | solution.py:44
  59.4 2.5 %collective-permute-start.20 = (f32[24,128]{1,0:T(8,128)S(1)}, f32[24,128]{1,0:T(8,128)S(1)}, u32[]{:S(2)}, u32[]{:S(2)}) collective-permute-start(f32[24,128]{1,0:T(8,128)S(1)} %get-tuple-element.85), channel_id=1, source_target_pairs={{0,5},{1,6},{2,7},{3,0},{4,1},{5,2},{6,3},{7,4},{8,13},{9,14},{10,... | collective-permute-start | bytes 36872 | tf_op jit(solution)/shard_map/ppermute | solution.py:44
  61.9 2.5 %collective-permute-start.19 = (f32[24,128]{1,0:T(8,128)S(1)}, f32[24,128]{1,0:T(8,128)S(1)}, u32[]{:S(2)}, u32[]{:S(2)}) collective-permute-start(f32[24,128]{1,0:T(8,128)S(1)} %get-tuple-element.84.refs_5_), channel_id=1, source_target_pairs={{0,3},{1,4},{2,5},{3,6},{4,7},{5,0},{6,1},{7,2},{8,11},{9,12},{10,... | collective-permute-start | bytes 36872 | tf_op jit(solution)/shard_map/ppermute | solution.py:44
  64.4 0.8 collective-permute-start.26
  65.2 0.6 collective-permute-start.25
  65.8 1.0 collective-permute-start.24
  66.8 1.4 %collective-permute-done.26.refs_11_ = f32[16,128]{1,0:T(8,128)S(1)} collective-permute-done((f32[16,128]{1,0:T(8,128)S(1)}, f32[16,128]{1,0:T(8,128)S(1)}, u32[]{:S(2)}, u32[]{:S(2)}) %collective-permute-start.26) | collective-permute-done | bytes 8224 | tf_op jit(solution)/shard_map/ppermute | solution.py:44
  68.1 2.2 %collective-permute-done.25.refs_10_ = f32[16,128]{1,0:T(8,128)S(1)} collective-permute-done((f32[16,128]{1,0:T(8,128)S(1)}, f32[16,128]{1,0:T(8,128)S(1)}, u32[]{:S(2)}, u32[]{:S(2)}) %collective-permute-start.25) | collective-permute-done | bytes 8224 | tf_op jit(solution)/shard_map/ppermute | solution.py:44
  70.3 0.5 collective-permute-done.24.refs_9_
  70.8 2.8 %grad_img0.1 = (bf16[528,1280]{1,0:T(8,128)(2,1)S(1)}, bf16[512,1024]{1,0:T(8,128)(2,1)S(1)}, f32[8,128]{1,0:T(8,128)S(1)}) custom-call(s32[16]{0:T(128)S(1)} %get-tuple-element.88.refs_0_, s32[16]{0:T(128)S(1)} %get-tuple-element.89.refs_1_, f32[2]{0:T(128)S(1)} %pad_maximum_fusion.2.refs_2_.scale_ref, f32[1024,1024]{1,0:T(8,128)S(1)} %get-tuple-element.49.refs_3_, ...), custom_call_target="tpu_custom_call" | custom-call | flops 1342177280 | bytes 1048576 | tf_op jit(solution)/shard_map/grad_img0/pallas_call | solution.py:342
  73.6 0.1 collective-permute-start.27
  73.7 2.8 %grad_img1.1 = (bf16[528,1280]{1,0:T(8,128)(2,1)S(1)}, bf16[512,1024]{1,0:T(8,128)(2,1)S(1)}) custom-call(s32[16]{0:T(128)S(1)} %get-tuple-element.88.refs_0_, s32[16]{0:T(128)S(1)} %get-tuple-element.89.refs_1_, f32[2]{0:T(128)S(1)} %pad_maximum_fusion.2.refs_2_.scale_ref, f32[1024,1024]{1,0:T(8,128)S(1)} %get-tuple-element.49.refs_3_, ...), custom_call_target="tpu_custom_call" | custom-call | flops 1342177280 | bytes 1048576 | tf_op jit(solution)/shard_map/grad_img1/pallas_call | solution.py:342
  76.5 0.3 collective-permute-done.27.arrived_ref
  76.8 0.4 pair.1
  77.1 2.3 %collective-permute-start.28 = (bf16[80,1280]{1,0:T(8,128)(2,1)S(1)}, bf16[80,1280]{1,0:T(8,128)(2,1)S(1)}, u32[]{:S(2)}, u32[]{:S(2)}) collective-permute-start(bf16[80,1280]{1,0:T(8,128)(2,1)S(1)} %get-tuple-element.57), channel_id=1, source_target_pairs={{0,7},{1,0},{2,1},{3,2},{4,3},{5,4},{6,5},{7,6},{8,15},{9,8},{10,9... | collective-permute-start | bytes 614408 | tf_op jit(solution)/shard_map/ppermute | solution.py:44
  79.5 3.8 %grad_txt.1 = (bf16[256,1280]{1,0:T(8,128)(2,1)S(1)}, bf16[256,1280]{1,0:T(8,128)(2,1)S(1)}, bf16[256,1280]{1,0:T(8,128)(2,1)S(1)}, bf16[144,1280]{1,0:T(8,128)(2,1)S(1)}, bf16[128,1280]{1,0:T(8,128)(2,1)S(1)}) custom-call(bf16[512,1024]{1,0:T(8,128)(2,1)S(1)} %get-tuple-element.58.low_ref, bf16[512,1024]{1,0:T(8,128)(2,1)S(1)} %get-tuple-element.59.high_ref, ...), custom_call_target="tpu_custom_call" | custom-call | flops 2684354560 | bytes 1048576 | tf_op jit(solution)/shard_map/grad_txt/pallas_call | solution.py:369
  83.4 2.9 %collective-permute-start.29 = (bf16[144,1280]{1,0:T(8,128)(2,1)S(1)}, bf16[144,1280]{1,0:T(8,128)(2,1)S(1)}, u32[]{:S(2)}, u32[]{:S(2)}) collective-permute-start(bf16[144,1280]{1,0:T(8,128)(2,1)S(1)} %ring_fold.3), channel_id=1, source_target_pairs={{0,7},{1,0},{2,1},{3,2},{4,3},{5,4},{6,5},{7,6},{8,15},{9,8},{10,9... | collective-permute-start | bytes 1105928 | tf_op jit(solution)/shard_map/ppermute | solution.py:44
  86.3 2.0 %collective-permute-start.30 = (bf16[144,1280]{1,0:T(8,128)(2,1)S(1)}, bf16[144,1280]{1,0:T(8,128)(2,1)S(1)}, u32[]{:S(2)}, u32[]{:S(2)}) collective-permute-start(bf16[144,1280]{1,0:T(8,128)(2,1)S(1)} %get-tuple-element.66), channel_id=1, source_target_pairs={{0,192},{1,193},{2,194},{3,195},{4,196},{5,197},{6,198},{7,199},{8... | collective-permute-start | bytes 1105928 | tf_op jit(solution)/shard_map/ppermute | solution.py:44
  88.3 8.3 %collective-permute-done.31.high_ref = bf16[128,1280]{1,0:T(8,128)(2,1)S(1)} collective-permute-done((bf16[128,1280]{1,0:T(8,128)(2,1)S(1)}, bf16[128,1280]{1,0:T(8,128)(2,1)S(1)}, u32[]{:S(2)}, u32[]{:S(2)}) %collective-permute-start.31) | collective-permute-done | bytes 327712 | tf_op jit(solution)/shard_map/ppermute | solution.py:44
  96.6 0.2 plane_fold.1
  96.8 0.5 collective-permute-start.33
  97.3 1.6 %collective-permute-start.34 = (bf16[272,1280]{1,0:T(8,128)(2,1)S(1)}, bf16[272,1280]{1,0:T(8,128)(2,1)S(1)}, u32[]{:S(2)}, u32[]{:S(2)}) collective-permute-start(bf16[272,1280]{1,0:T(8,128)(2,1)S(1)} %get-tuple-element.74), channel_id=1, source_target_pairs={{0,64},{1,65},{2,66},{3,67},{4,68},{5,69},{6,70},{7,71},{8,72},{9,... | collective-permute-start | bytes 2088968 | tf_op jit(solution)/shard_map/ppermute | solution.py:44
  99.0 3.2 %collective-permute-start.32 = (bf16[144,1280]{1,0:T(8,128)(2,1)S(1)}, bf16[144,1280]{1,0:T(8,128)(2,1)S(1)}, u32[]{:S(2)}, u32[]{:S(2)}) collective-permute-start(bf16[144,1280]{1,0:T(8,128)(2,1)S(1)} %ring_fold.4), channel_id=1, source_target_pairs={{0,7},{1,0},{2,1},{3,2},{4,3},{5,4},{6,5},{7,6},{8,15},{9,8},{10,9... | collective-permute-start | bytes 1105928 | tf_op jit(solution)/shard_map/ppermute | solution.py:44
  102.2 5.0 %collective-permute-done.32.refs_1_ = bf16[144,1280]{1,0:T(8,128)(2,1)S(1)} collective-permute-done((bf16[144,1280]{1,0:T(8,128)(2,1)S(1)}, bf16[144,1280]{1,0:T(8,128)(2,1)S(1)}, u32[]{:S(2)}, u32[]{:S(2)}) %collective-permute-start.32) | collective-permute-done | bytes 368672 | tf_op jit(solution)/shard_map/ppermute | solution.py:44
  107.2 0.7 collective-permute-done.33.down_ref
  107.9 1.6 %collective-permute-done.34.up_ref = bf16[272,1280]{1,0:T(8,128)(2,1)S(1)} collective-permute-done((bf16[272,1280]{1,0:T(8,128)(2,1)S(1)}, bf16[272,1280]{1,0:T(8,128)(2,1)S(1)}, u32[]{:S(2)}, u32[]{:S(2)}) %collective-permute-start.34) | collective-permute-done | bytes 696352 | tf_op jit(solution)/shard_map/ppermute | solution.py:44
  109.5 0.1 ring_fold.5
  109.7 3.2 %collective-permute-start.35 = (bf16[144,1280]{1,0:T(8,128)(2,1)S(1)}, bf16[144,1280]{1,0:T(8,128)(2,1)S(1)}, u32[]{:S(2)}, u32[]{:S(2)}) collective-permute-start(bf16[144,1280]{1,0:T(8,128)(2,1)S(1)} %ring_fold.5), channel_id=1, source_target_pairs={{0,7},{1,0},{2,1},{3,2},{4,3},{5,4},{6,5},{7,6},{8,15},{9,8},{10,9... | collective-permute-start | bytes 1105928 | tf_op jit(solution)/shard_map/ppermute | solution.py:44
  112.8 0.2 line.1
  113.1 6.5 %collective-permute-start.37 = (bf16[80,1280]{1,0:T(8,128)(2,1)S(1)}, bf16[80,1280]{1,0:T(8,128)(2,1)S(1)}, u32[]{:S(2)}, u32[]{:S(2)}) collective-permute-start(bf16[80,1280]{1,0:T(8,128)(2,1)S(1)} %get-tuple-element.80), channel_id=1, source_target_pairs={{0,40},{1,41},{2,42},{3,43},{4,44},{5,45},{6,46},{7,47},{8,0},{9,1... | collective-permute-start | bytes 614408 | tf_op jit(solution)/shard_map/ppermute | solution.py:44
  119.6 2.3 %collective-permute-start.39 = (bf16[80,1280]{1,0:T(8,128)(2,1)S(1)}, bf16[80,1280]{1,0:T(8,128)(2,1)S(1)}, u32[]{:S(2)}, u32[]{:S(2)}) collective-permute-start(bf16[80,1280]{1,0:T(8,128)(2,1)S(1)} %get-tuple-element.82), channel_id=1, source_target_pairs={{0,32},{1,33},{2,34},{3,35},{4,36},{5,37},{6,38},{7,39},{8,40},{9,... | collective-permute-start | bytes 614408 | tf_op jit(solution)/shard_map/ppermute | solution.py:44
  121.9 0.1 collective-permute-start.36
  122.0 1.3 collective-permute-done.37.refs_4_
  123.2 5.5 %collective-permute-done.38.refs_5_ = bf16[80,1280]{1,0:T(8,128)(2,1)S(1)} collective-permute-done((bf16[80,1280]{1,0:T(8,128)(2,1)S(1)}, bf16[80,1280]{1,0:T(8,128)(2,1)S(1)}, u32[]{:S(2)}, u32[]{:S(2)}) %collective-permute-start.38) | collective-permute-done | bytes 204832 | tf_op jit(solution)/shard_map/ppermute | solution.py:44
  128.7 1.7 %finish.1 = (bf16[64,1280]{1,0:T(8,128)(2,1)}, bf16[64,1280]{1,0:T(8,128)(2,1)}, f32[1]{0:T(128)}, f32[1]{0:T(128)}) custom-call(f32[2]{0:T(128)S(1)} %pad_maximum_fusion.2.refs_2_.scale_ref, bf16[64,1280]{1,0:T(8,128)(2,1)S(1)} %copy-done.1, bf16[64,1280]{1,0:T(8,128)(2,1)S(1)} %copy-done.3, bf16[64,1280]{1,0:T(8,128)(2,1)S(1)} %get-tuple-element.44.refs_13_.img_hat_ref, ...), custom_call_target="tpu_custom_call" | custom-call | bytes 1048576 | tf_op jit(solution)/shard_map/finish/pallas_call | solution.py:405
  (56 shorter events, 1.0 us)
Async XLA Ops:
  0.6 30.9 %copy-start.4 = (s32[4]{0:T(128)S(1)}, s32[4]{0:T(128)}, u32[]{:S(2)}) copy-start(s32[4]{0:T(128)} %constant.86.clone) | copy-start | bytes 52
  0.6 0.9 copy-start
  1.6 0.9 copy-start.2
  2.9 5.2 %collective-permute-start = (bf16[64,1280]{1,0:T(8,128)(2,1)S(1)}, bf16[64,1280]{1,0:T(8,128)(2,1)S(1)}, u32[]{:S(2)}, u32[]{:S(2)}) collective-permute-start(bf16[64,1280]{1,0:T(8,128)(2,1)S(1)} %get-tuple-element.44.refs_13_.img_hat_ref), channel_id=1, source_target_pairs={{0,16},{1,17},{2,18},{3,19},{4,20},{5,21},{6,22},{7,23},{8,24},{9,... | collective-permute-start | bytes 491528 | tf_op jit(solution)/shard_map/ppermute | solution.py:44
  3.0 6.9 %collective-permute-start.4 = (bf16[64,1280]{1,0:T(8,128)(2,1)S(1)}, bf16[64,1280]{1,0:T(8,128)(2,1)S(1)}, u32[]{:S(2)}, u32[]{:S(2)}) collective-permute-start(bf16[64,1280]{1,0:T(8,128)(2,1)S(1)} %get-tuple-element.45.txt_hat_ref), channel_id=1, source_target_pairs={{0,32},{1,33},{2,34},{3,35},{4,36},{5,37},{6,38},{7,39},{8,40},{9,... | collective-permute-start | bytes 491528 | tf_op jit(solution)/shard_map/ppermute | solution.py:44
  6.1 5.6 %collective-permute-start.3 = (bf16[64,1280]{1,0:T(8,128)(2,1)S(1)}, bf16[64,1280]{1,0:T(8,128)(2,1)S(1)}, u32[]{:S(2)}, u32[]{:S(2)}) collective-permute-start(bf16[64,1280]{1,0:T(8,128)(2,1)S(1)} %get-tuple-element.45.txt_hat_ref), channel_id=1, source_target_pairs={{0,40},{1,41},{2,42},{3,43},{4,44},{5,45},{6,46},{7,47},{8,0},{9,1... | collective-permute-start | bytes 491528 | tf_op jit(solution)/shard_map/ppermute | solution.py:44
  7.2 6.5 %collective-permute-start.2 = (bf16[64,1280]{1,0:T(8,128)(2,1)S(1)}, bf16[64,1280]{1,0:T(8,128)(2,1)S(1)}, u32[]{:S(2)}, u32[]{:S(2)}) collective-permute-start(bf16[64,1280]{1,0:T(8,128)(2,1)S(1)} %get-tuple-element.45.txt_hat_ref), channel_id=1, source_target_pairs={{0,8},{1,9},{2,10},{3,11},{4,12},{5,13},{6,14},{7,15},{8,32},{9,33... | collective-permute-start | bytes 491528 | tf_op jit(solution)/shard_map/ppermute | solution.py:44
  8.1 30.3 %copy-start.5 = (s32[16]{0:T(128)S(1)}, s32[16]{0:T(128)}, u32[]{:S(2)}) copy-start(s32[16]{0:T(128)} %constant.88.clone) | copy-start | bytes 196
  8.1 30.3 %copy-start.6 = (s32[16]{0:T(128)S(1)}, s32[16]{0:T(128)}, u32[]{:S(2)}) copy-start(s32[16]{0:T(128)} %constant.87.clone) | copy-start | bytes 196
  8.2 7.2 %collective-permute-start.1 = (bf16[128,1280]{1,0:T(8,128)(2,1)S(1)}, bf16[128,1280]{1,0:T(8,128)(2,1)S(1)}, u32[]{:S(2)}, u32[]{:S(2)}) collective-permute-start(bf16[128,1280]{1,0:T(8,128)(2,1)S(1)} %pad_maximum_fusion.1), channel_id=1, source_target_pairs={{0,1},{1,2},{2,3},{3,4},{4,5},{5,6},{6,7},{7,0},{8,9},{9,10},{10,1... | collective-permute-start | bytes 983048 | tf_op jit(solution)/shard_map/ppermute | solution.py:44
  15.3 7.3 %collective-permute-start.6 = (bf16[128,1280]{1,0:T(8,128)(2,1)S(1)}, bf16[128,1280]{1,0:T(8,128)(2,1)S(1)}, u32[]{:S(2)}, u32[]{:S(2)}) collective-permute-start(bf16[128,1280]{1,0:T(8,128)(2,1)S(1)} %collective-permute-done.1.refs_9_), channel_id=1, source_target_pairs={{0,1},{1,2},{2,3},{3,4},{4,5},{5,6},{6,7},{7,0},{8,9},{9,10},{10,1... | collective-permute-start | bytes 983048 | tf_op jit(solution)/shard_map/ppermute | solution.py:44
  16.3 15.5 %collective-permute-start.13 = (bf16[256,1280]{1,0:T(8,128)(2,1)S(1)}, bf16[256,1280]{1,0:T(8,128)(2,1)S(1)}, u32[]{:S(2)}, u32[]{:S(2)}) collective-permute-start(bf16[256,1280]{1,0:T(8,128)(2,1)S(1)} %pad_maximum_fusion.refs_14_), channel_id=1, source_target_pairs={{0,192},{1,193},{2,194},{3,195},{4,196},{5,197},{6,198},{7,199},{8... | collective-permute-start | bytes 1966088 | tf_op jit(solution)/shard_map/ppermute | solution.py:44
  19.3 13.0 %collective-permute-start.12 = (bf16[256,1280]{1,0:T(8,128)(2,1)S(1)}, bf16[256,1280]{1,0:T(8,128)(2,1)S(1)}, u32[]{:S(2)}, u32[]{:S(2)}) collective-permute-start(bf16[256,1280]{1,0:T(8,128)(2,1)S(1)} %pad_maximum_fusion.refs_14_), channel_id=1, source_target_pairs={{0,64},{1,65},{2,66},{3,67},{4,68},{5,69},{6,70},{7,71},{8,72},{9,... | collective-permute-start | bytes 1966088 | tf_op jit(solution)/shard_map/ppermute | solution.py:44
  22.6 8.3 %collective-permute-start.8 = (bf16[128,1280]{1,0:T(8,128)(2,1)S(1)}, bf16[128,1280]{1,0:T(8,128)(2,1)S(1)}, u32[]{:S(2)}, u32[]{:S(2)}) collective-permute-start(bf16[128,1280]{1,0:T(8,128)(2,1)S(1)} %collective-permute-done.6.refs_10_), channel_id=1, source_target_pairs={{0,1},{1,2},{2,3},{3,4},{4,5},{5,6},{6,7},{7,0},{8,9},{9,10},{10,1... | collective-permute-start | bytes 983048 | tf_op jit(solution)/shard_map/ppermute | solution.py:44
  23.4 12.1 %collective-permute-start.5 = (bf16[128,1280]{1,0:T(8,128)(2,1)S(1)}, bf16[128,1280]{1,0:T(8,128)(2,1)}, u32[]{:S(2)}, u32[]{:S(2)}) collective-permute-start(bf16[128,1280]{1,0:T(8,128)(2,1)S(1)} %collective-permute-done.1.refs_9_), channel_id=1, source_target_pairs={{0,16},{1,17},{2,18},{3,19},{4,20},{5,21},{6,22},{7,23},{8,24},{9,... | collective-permute-start | bytes 983048 | tf_op jit(solution)/shard_map/ppermute | solution.py:44
  31.5 6.8 %collective-permute-start.10 = (bf16[64,1280]{1,0:T(8,128)(2,1)}, bf16[64,1280]{1,0:T(8,128)(2,1)}, u32[]{:S(2)}, u32[]{:S(2)}) collective-permute-start(bf16[64,1280]{1,0:T(8,128)(2,1)} %slice.16), channel_id=1, source_target_pairs={{0,1},{1,2},{2,3},{3,4},{4,5},{5,6},{6,7},{7,0},{8,9},{9,10},{10,1... | collective-permute-start | bytes 491528 | tf_op jit(solution)/shard_map/ppermute | solution.py:44
  31.8 7.4 %collective-permute-start.7 = (bf16[128,1280]{1,0:T(8,128)(2,1)S(1)}, bf16[128,1280]{1,0:T(8,128)(2,1)S(1)}, u32[]{:S(2)}, u32[]{:S(2)}) collective-permute-start(bf16[128,1280]{1,0:T(8,128)(2,1)S(1)} %collective-permute-done.6.refs_10_), channel_id=1, source_target_pairs={{0,16},{1,17},{2,18},{3,19},{4,20},{5,21},{6,22},{7,23},{8,24},{9,... | collective-permute-start | bytes 983048 | tf_op jit(solution)/shard_map/ppermute | solution.py:44
  31.8 8.2 %collective-permute-start.9 = (bf16[128,1280]{1,0:T(8,128)(2,1)S(1)}, bf16[128,1280]{1,0:T(8,128)(2,1)S(1)}, u32[]{:S(2)}, u32[]{:S(2)}) collective-permute-start(bf16[128,1280]{1,0:T(8,128)(2,1)S(1)} %collective-permute-done.8.refs_11_), channel_id=1, source_target_pairs={{0,16},{1,17},{2,18},{3,19},{4,20},{5,21},{6,22},{7,23},{8,24},{9,... | collective-permute-start | bytes 983048 | tf_op jit(solution)/shard_map/ppermute | solution.py:44
  32.4 7.7 %collective-permute-start.15 = (bf16[128,1280]{1,0:T(8,128)(2,1)S(1)}, bf16[128,1280]{1,0:T(8,128)(2,1)S(1)}, u32[]{:S(2)}, u32[]{:S(2)}) collective-permute-start(bf16[128,1280]{1,0:T(8,128)(2,1)S(1)} %slice.18), channel_id=1, source_target_pairs={{0,192},{1,193},{2,194},{3,195},{4,196},{5,197},{6,198},{7,199},{8... | collective-permute-start | bytes 983048 | tf_op jit(solution)/shard_map/ppermute | solution.py:44
  35.5 8.4 %collective-permute-start.14 = (bf16[128,1280]{1,0:T(8,128)(2,1)S(1)}, bf16[128,1280]{1,0:T(8,128)(2,1)S(1)}, u32[]{:S(2)}, u32[]{:S(2)}) collective-permute-start(bf16[128,1280]{1,0:T(8,128)(2,1)S(1)} %slice.17), channel_id=1, source_target_pairs={{0,64},{1,65},{2,66},{3,67},{4,68},{5,69},{6,70},{7,71},{8,72},{9,... | collective-permute-start | bytes 983048 | tf_op jit(solution)/shard_map/ppermute | solution.py:44
  38.4 1.6 %collective-permute-start.11 = (bf16[64,1280]{1,0:T(8,128)(2,1)}, bf16[64,1280]{1,0:T(8,128)(2,1)S(1)}, u32[]{:S(2)}, u32[]{:S(2)}) collective-permute-start(bf16[64,1280]{1,0:T(8,128)(2,1)} %collective-permute-done.10.refs_12_), channel_id=1, source_target_pairs={{0,16},{1,17},{2,18},{3,19},{4,20},{5,21},{6,22},{7,23},{8,24},{9,... | collective-permute-start | bytes 491528 | tf_op jit(solution)/shard_map/ppermute | solution.py:44
  49.9 1.3 collective-permute-start.16
  51.2 6.5 %collective-permute-start.18 = (f32[24,128]{1,0:T(8,128)S(1)}, f32[24,128]{1,0:T(8,128)S(1)}, u32[]{:S(2)}, u32[]{:S(2)}) collective-permute-start(f32[24,128]{1,0:T(8,128)S(1)} %add.94), channel_id=1, source_target_pairs={{0,7},{1,0},{2,1},{3,2},{4,3},{5,4},{6,5},{7,6},{8,15},{9,8},{10,9... | collective-permute-start | bytes 36872 | tf_op jit(solution)/shard_map/ppermute | solution.py:44
  54.4 4.9 %collective-permute-start.17 = (f32[24,128]{1,0:T(8,128)S(1)}, f32[24,128]{1,0:T(8,128)S(1)}, u32[]{:S(2)}, u32[]{:S(2)}) collective-permute-start(f32[24,128]{1,0:T(8,128)S(1)} %add.94), channel_id=1, source_target_pairs={{0,1},{1,2},{2,3},{3,4},{4,5},{5,6},{6,7},{7,0},{8,9},{9,10},{10,1... | collective-permute-start | bytes 36872 | tf_op jit(solution)/shard_map/ppermute | solution.py:44
  54.4 9.9 %collective-permute-start.23 = (f32[16,128]{1,0:T(8,128)S(1)}, f32[16,128]{1,0:T(8,128)S(1)}, u32[]{:S(2)}, u32[]{:S(2)}) collective-permute-start(f32[16,128]{1,0:T(8,128)S(1)} %get-tuple-element.52), channel_id=1, source_target_pairs={{0,40},{1,41},{2,42},{3,43},{4,44},{5,45},{6,46},{7,47},{8,0},{9,1... | collective-permute-start | bytes 24584 | tf_op jit(solution)/shard_map/ppermute | solution.py:44
  56.8 7.6 %collective-permute-start.22 = (f32[16,128]{1,0:T(8,128)S(1)}, f32[16,128]{1,0:T(8,128)S(1)}, u32[]{:S(2)}, u32[]{:S(2)}) collective-permute-start(f32[16,128]{1,0:T(8,128)S(1)} %get-tuple-element.52), channel_id=1, source_target_pairs={{0,32},{1,33},{2,34},{3,35},{4,36},{5,37},{6,38},{7,39},{8,40},{9,... | collective-permute-start | bytes 24584 | tf_op jit(solution)/shard_map/ppermute | solution.py:44
  57.1 7.3 %collective-permute-start.21 = (f32[16,128]{1,0:T(8,128)S(1)}, f32[16,128]{1,0:T(8,128)S(1)}, u32[]{:S(2)}, u32[]{:S(2)}) collective-permute-start(f32[16,128]{1,0:T(8,128)S(1)} %get-tuple-element.52), channel_id=1, source_target_pairs={{0,8},{1,9},{2,10},{3,11},{4,12},{5,13},{6,14},{7,15},{8,32},{9,33... | collective-permute-start | bytes 24584 | tf_op jit(solution)/shard_map/ppermute | solution.py:44
  59.4 11.5 %collective-permute-start.20 = (f32[24,128]{1,0:T(8,128)S(1)}, f32[24,128]{1,0:T(8,128)S(1)}, u32[]{:S(2)}, u32[]{:S(2)}) collective-permute-start(f32[24,128]{1,0:T(8,128)S(1)} %get-tuple-element.85), channel_id=1, source_target_pairs={{0,5},{1,6},{2,7},{3,0},{4,1},{5,2},{6,3},{7,4},{8,13},{9,14},{10,... | collective-permute-start | bytes 36872 | tf_op jit(solution)/shard_map/ppermute | solution.py:44
  61.9 8.9 %collective-permute-start.19 = (f32[24,128]{1,0:T(8,128)S(1)}, f32[24,128]{1,0:T(8,128)S(1)}, u32[]{:S(2)}, u32[]{:S(2)}) collective-permute-start(f32[24,128]{1,0:T(8,128)S(1)} %get-tuple-element.84.refs_5_), channel_id=1, source_target_pairs={{0,3},{1,4},{2,5},{3,6},{4,7},{5,0},{6,1},{7,2},{8,11},{9,12},{10,... | collective-permute-start | bytes 36872 | tf_op jit(solution)/shard_map/ppermute | solution.py:44
  64.4 3.7 %collective-permute-start.26 = (f32[16,128]{1,0:T(8,128)S(1)}, f32[16,128]{1,0:T(8,128)S(1)}, u32[]{:S(2)}, u32[]{:S(2)}) collective-permute-start(f32[16,128]{1,0:T(8,128)S(1)} %add_add_fusion.refs_8_), channel_id=1, source_target_pairs={{0,192},{1,193},{2,194},{3,195},{4,196},{5,197},{6,198},{7,199},{8... | collective-permute-start | bytes 24584 | tf_op jit(solution)/shard_map/ppermute | solution.py:44
  65.2 5.2 %collective-permute-start.25 = (f32[16,128]{1,0:T(8,128)S(1)}, f32[16,128]{1,0:T(8,128)S(1)}, u32[]{:S(2)}, u32[]{:S(2)}) collective-permute-start(f32[16,128]{1,0:T(8,128)S(1)} %add_add_fusion.refs_8_), channel_id=1, source_target_pairs={{0,128},{1,129},{2,130},{3,131},{4,132},{5,133},{6,134},{7,135},{8... | collective-permute-start | bytes 24584 | tf_op jit(solution)/shard_map/ppermute | solution.py:44
  65.8 5.0 %collective-permute-start.24 = (f32[16,128]{1,0:T(8,128)S(1)}, f32[16,128]{1,0:T(8,128)S(1)}, u32[]{:S(2)}, u32[]{:S(2)}) collective-permute-start(f32[16,128]{1,0:T(8,128)S(1)} %add_add_fusion.refs_8_), channel_id=1, source_target_pairs={{0,64},{1,65},{2,66},{3,67},{4,68},{5,69},{6,70},{7,71},{8,72},{9,... | collective-permute-start | bytes 24584 | tf_op jit(solution)/shard_map/ppermute | solution.py:44
  73.6 3.2 %collective-permute-start.27 = (bf16[528,1280]{1,0:T(8,128)(2,1)S(1)}, bf16[528,1280]{1,0:T(8,128)(2,1)S(1)}, u32[]{:S(2)}, u32[]{:S(2)}) collective-permute-start(bf16[528,1280]{1,0:T(8,128)(2,1)S(1)} %get-tuple-element.54), channel_id=1, source_target_pairs={{0,16},{1,17},{2,18},{3,19},{4,20},{5,21},{6,22},{7,23},{8,24},{9,... | collective-permute-start | bytes 4055048 | tf_op jit(solution)/shard_map/ppermute | solution.py:44
  77.1 6.2 %collective-permute-start.28 = (bf16[80,1280]{1,0:T(8,128)(2,1)S(1)}, bf16[80,1280]{1,0:T(8,128)(2,1)S(1)}, u32[]{:S(2)}, u32[]{:S(2)}) collective-permute-start(bf16[80,1280]{1,0:T(8,128)(2,1)S(1)} %get-tuple-element.57), channel_id=1, source_target_pairs={{0,7},{1,0},{2,1},{3,2},{4,3},{5,4},{6,5},{7,6},{8,15},{9,8},{10,9... | collective-permute-start | bytes 614408 | tf_op jit(solution)/shard_map/ppermute | solution.py:44
  83.4 13.2 %collective-permute-start.29 = (bf16[144,1280]{1,0:T(8,128)(2,1)S(1)}, bf16[144,1280]{1,0:T(8,128)(2,1)S(1)}, u32[]{:S(2)}, u32[]{:S(2)}) collective-permute-start(bf16[144,1280]{1,0:T(8,128)(2,1)S(1)} %ring_fold.3), channel_id=1, source_target_pairs={{0,7},{1,0},{2,1},{3,2},{4,3},{5,4},{6,5},{7,6},{8,15},{9,8},{10,9... | collective-permute-start | bytes 1105928 | tf_op jit(solution)/shard_map/ppermute | solution.py:44
  86.3 10.3 %collective-permute-start.30 = (bf16[144,1280]{1,0:T(8,128)(2,1)S(1)}, bf16[144,1280]{1,0:T(8,128)(2,1)S(1)}, u32[]{:S(2)}, u32[]{:S(2)}) collective-permute-start(bf16[144,1280]{1,0:T(8,128)(2,1)S(1)} %get-tuple-element.66), channel_id=1, source_target_pairs={{0,192},{1,193},{2,194},{3,195},{4,196},{5,197},{6,198},{7,199},{8... | collective-permute-start | bytes 1105928 | tf_op jit(solution)/shard_map/ppermute | solution.py:44
  88.3 8.3 %collective-permute-start.31 = (bf16[128,1280]{1,0:T(8,128)(2,1)S(1)}, bf16[128,1280]{1,0:T(8,128)(2,1)S(1)}, u32[]{:S(2)}, u32[]{:S(2)}) collective-permute-start(bf16[128,1280]{1,0:T(8,128)(2,1)S(1)} %get-tuple-element.67), channel_id=1, source_target_pairs={{0,64},{1,65},{2,66},{3,67},{4,68},{5,69},{6,70},{7,71},{8,72},{9,... | collective-permute-start | bytes 983048 | tf_op jit(solution)/shard_map/ppermute | solution.py:44
  96.8 11.1 %collective-permute-start.33 = (bf16[272,1280]{1,0:T(8,128)(2,1)S(1)}, bf16[272,1280]{1,0:T(8,128)(2,1)S(1)}, u32[]{:S(2)}, u32[]{:S(2)}) collective-permute-start(bf16[272,1280]{1,0:T(8,128)(2,1)S(1)} %get-tuple-element.73), channel_id=1, source_target_pairs={{0,192},{1,193},{2,194},{3,195},{4,196},{5,197},{6,198},{7,199},{8... | collective-permute-start | bytes 2088968 | tf_op jit(solution)/shard_map/ppermute | solution.py:44
  97.3 12.2 %collective-permute-start.34 = (bf16[272,1280]{1,0:T(8,128)(2,1)S(1)}, bf16[272,1280]{1,0:T(8,128)(2,1)S(1)}, u32[]{:S(2)}, u32[]{:S(2)}) collective-permute-start(bf16[272,1280]{1,0:T(8,128)(2,1)S(1)} %get-tuple-element.74), channel_id=1, source_target_pairs={{0,64},{1,65},{2,66},{3,67},{4,68},{5,69},{6,70},{7,71},{8,72},{9,... | collective-permute-start | bytes 2088968 | tf_op jit(solution)/shard_map/ppermute | solution.py:44
  99.0 8.2 %collective-permute-start.32 = (bf16[144,1280]{1,0:T(8,128)(2,1)S(1)}, bf16[144,1280]{1,0:T(8,128)(2,1)S(1)}, u32[]{:S(2)}, u32[]{:S(2)}) collective-permute-start(bf16[144,1280]{1,0:T(8,128)(2,1)S(1)} %ring_fold.4), channel_id=1, source_target_pairs={{0,7},{1,0},{2,1},{3,2},{4,3},{5,4},{6,5},{7,6},{8,15},{9,8},{10,9... | collective-permute-start | bytes 1105928 | tf_op jit(solution)/shard_map/ppermute | solution.py:44
  109.6 19.1 %copy-start.1 = (bf16[64,1280]{1,0:T(8,128)(2,1)S(1)}, bf16[64,1280]{1,0:T(8,128)(2,1)}, u32[]{:S(2)}) copy-start(bf16[64,1280]{1,0:T(8,128)(2,1)} %img_ref.3) | copy-start | bytes 491524
  109.6 19.1 %copy-start.3 = (bf16[64,1280]{1,0:T(8,128)(2,1)S(1)}, bf16[64,1280]{1,0:T(8,128)(2,1)}, u32[]{:S(2)}) copy-start(bf16[64,1280]{1,0:T(8,128)(2,1)} %txt_ref.3) | copy-start | bytes 491524
  109.7 12.2 %collective-permute-start.35 = (bf16[144,1280]{1,0:T(8,128)(2,1)S(1)}, bf16[144,1280]{1,0:T(8,128)(2,1)S(1)}, u32[]{:S(2)}, u32[]{:S(2)}) collective-permute-start(bf16[144,1280]{1,0:T(8,128)(2,1)S(1)} %ring_fold.5), channel_id=1, source_target_pairs={{0,7},{1,0},{2,1},{3,2},{4,3},{5,4},{6,5},{7,6},{8,15},{9,8},{10,9... | collective-permute-start | bytes 1105928 | tf_op jit(solution)/shard_map/ppermute | solution.py:44
  113.1 10.2 %collective-permute-start.37 = (bf16[80,1280]{1,0:T(8,128)(2,1)S(1)}, bf16[80,1280]{1,0:T(8,128)(2,1)S(1)}, u32[]{:S(2)}, u32[]{:S(2)}) collective-permute-start(bf16[80,1280]{1,0:T(8,128)(2,1)S(1)} %get-tuple-element.80), channel_id=1, source_target_pairs={{0,40},{1,41},{2,42},{3,43},{4,44},{5,45},{6,46},{7,47},{8,0},{9,1... | collective-permute-start | bytes 614408 | tf_op jit(solution)/shard_map/ppermute | solution.py:44
  119.6 9.2 %collective-permute-start.38 = (bf16[80,1280]{1,0:T(8,128)(2,1)S(1)}, bf16[80,1280]{1,0:T(8,128)(2,1)S(1)}, u32[]{:S(2)}, u32[]{:S(2)}) collective-permute-start(bf16[80,1280]{1,0:T(8,128)(2,1)S(1)} %get-tuple-element.81), channel_id=1, source_target_pairs={{0,8},{1,9},{2,10},{3,11},{4,12},{5,13},{6,14},{7,15},{8,32},{9,33... | collective-permute-start | bytes 614408 | tf_op jit(solution)/shard_map/ppermute | solution.py:44
  119.6 9.1 %collective-permute-start.39 = (bf16[80,1280]{1,0:T(8,128)(2,1)S(1)}, bf16[80,1280]{1,0:T(8,128)(2,1)S(1)}, u32[]{:S(2)}, u32[]{:S(2)}) collective-permute-start(bf16[80,1280]{1,0:T(8,128)(2,1)S(1)} %get-tuple-element.82), channel_id=1, source_target_pairs={{0,32},{1,33},{2,34},{3,35},{4,36},{5,37},{6,38},{7,39},{8,40},{9,... | collective-permute-start | bytes 614408 | tf_op jit(solution)/shard_map/ppermute | solution.py:44
  121.9 6.9 %collective-permute-start.36 = (bf16[80,1280]{1,0:T(8,128)(2,1)S(1)}, bf16[80,1280]{1,0:T(8,128)(2,1)S(1)}, u32[]{:S(2)}, u32[]{:S(2)}) collective-permute-start(bf16[80,1280]{1,0:T(8,128)(2,1)S(1)} %slice.19), channel_id=1, source_target_pairs={{0,16},{1,17},{2,18},{3,19},{4,20},{5,21},{6,22},{7,23},{8,24},{9,... | collective-permute-start | bytes 614408 | tf_op jit(solution)/shard_map/ppermute | solution.py:44
where the time goes:
time: 131 us
  waiting for transfers between devices  53.8 us (41%)
  starting transfers between devices  53.5 us (41%)
  Pallas kernels  18.6 us (14%)
  local copies, waits for them, and re-layouts  2.76 us (2%)
  between operations  1.76 us (1%)
    ppermute x40, waiting for transfers between devices, permute(): return lax.ppermute(array, AXES, pairs)  53.8 us
    ppermute x40, starting transfers between devices, permute(): return lax.ppermute(array, AXES, pairs)  53.5 us
    pallas_call x1, Pallas kernels, per_device(): call(lambda *refs: logits_kernel(counts, *refs), (shape(total, width), sh...  6.1 us
    pallas_call x2, Pallas kernels, grad_img(): call(lambda *refs: grad_img_kernel(half, *refs), (shape(total // 2 + 16,...  5.53 us
    pallas_call x1, Pallas kernels, per_device(): call(grad_txt_kernel, (shape(256, width),) * 3 + (shape(144, width), shap...  3.84 us
  transfers between devices with their start and end apart: 40, of which 21 were waited for; matrix products, arithmetic and copies ran while one was open for 1% of the time, Pallas kernels for 5%

commit v1 on v0

--- a/solution.py
+++ b/solution.py
@@ -113,6 +113,13 @@
     encode(out_ref, 128, scalar_ref[...] + decode(arrived_ref, rows))
 
 
+def last_fold_kernel(base_ref, arrived_ref, scalar_ref, own_ref, sib_ref):
+    for k, out in enumerate((own_ref, sib_ref)):
+        cut = slice(k * 64, (k + 1) * 64)
+        out[0:64, :] = (base_ref[cut, :].astype(F32) + arrived_ref[cut, :].astype(F32)).astype(BF16)
+    encode(sib_ref, 64, scalar_ref[...] + decode(arrived_ref, 128))
+
+
 def plane_fold_kernel(minus_ref, plus_ref, low_ref, high_ref, scalar_ref, to_minus_ref, to_plus_ref):
     to_minus_ref[0:128, :] = (minus_ref[0:128, :].astype(F32) + low_ref[0:128, :].astype(F32)).astype(BF16)
     to_minus_ref[128:256, :] = minus_ref[128:256, :]
@@ -134,9 +141,9 @@
     outs[4][...] = scalars
 
 
-def logits_kernel(counts, *refs):
+def logits_kernel(img_order, txt_order, *refs):
     row_place, col_place, scale_ref, diag_ref = refs[:4]
-    n_img, n_txt = len(counts[0]), len(counts[1])
+    n_img, n_txt = 9, 5
     img_refs, txt_refs = refs[4 : 4 + n_img], refs[4 + n_img : 4 + n_img + n_txt]
     img_all, txt_all, logit_ref, row_ref, col_ref, row_acc = refs[4 + n_img + n_txt :]
     step = pl.program_id(0)
@@ -144,10 +151,10 @@
 
     @pl.when(step == 0)
     def _():
-        for blocks, sizes, target in ((img_refs, counts[0], img_all), (txt_refs, counts[1], txt_all)):
+        for blocks, order, target in ((img_refs, img_order, img_all), (txt_refs, txt_order, txt_all)):
             at = 0
-            for block, size in zip(blocks, sizes):
-                target[at : at + size, :] = block[...]
+            for k, first, size in order:
+                target[at : at + size, :] = blocks[k][first : first + size, :]
                 at += size
         row_acc[...] = jnp.zeros_like(row_acc)
 
@@ -214,35 +221,38 @@
     grad_ref[pl.ds(start, tile), :] = jnp.dot(dlogit, txt_ref[...], preferred_element_type=F32).astype(BF16)
 
 
-def grad_txt_kernel(low_ref, high_ref, img_ref, scalar_ref, *outs):
-    step = pl.program_id(0)
-    tile = 256
-    start = pl.multiple_of(step * tile, tile)
-    grad = sum(
+def grad_txt_tile(start, low_ref, high_ref, img_ref):
+    return sum(
         lax.dot_general(
-            part[:, pl.ds(start, tile)],
+            part[:, pl.ds(start, 256)],
             img_ref[k * 512 : (k + 1) * 512, :],
             (((0,), (0,)), ((), ())),
             preferred_element_type=F32,
         )
         for k, part in enumerate((low_ref, high_ref))
     ).astype(BF16)
-    for k, ref in enumerate(outs[:3]):
+
+
+def grad_txt_far_kernel(low_ref, high_ref, img_ref, scalar_ref, far_low_ref, far_high_ref):
+    grad = grad_txt_tile(768, low_ref, high_ref, img_ref)
+    far_low_ref[0:128, :] = grad[0:128]
+    far_high_ref[...] = grad[128:256]
+    encode(far_low_ref, 128, scalar_ref[...])
+
+
+def grad_txt_kernel(low_ref, high_ref, img_ref, *outs):
+    step = pl.program_id(0)
+    grad = grad_txt_tile(pl.multiple_of(step * 256, 256), low_ref, high_ref, img_ref)
+    for k, ref in enumerate(outs):
 
         @pl.when(step == k)
         def _():
             ref[...] = grad
 
-    @pl.when(step == 3)
-    def _():
-        outs[3][0:128, :] = grad[0:128]
-        outs[4][...] = grad[128:256]
-        encode(outs[3], 128, scalar_ref[...])
-
 
 def finish_kernel(scale_ref, img_ref, txt_ref, img_hat_ref, txt_hat_ref, *refs):
-    own_img, ring_img, sib_img, own_txt, txt1, txt2, txt3, col_ref, row_ref = refs[:9]
-    grad_img_ref, grad_txt_ref, loss_ref, slope_ref = refs[9:]
+    own_img, ring_img, sib_img, for_sib, own_txt, txt1, txt2, txt3, col_ref, row_ref = refs[:10]
+    grad_img_ref, grad_txt_ref, loss_ref, slope_ref = refs[10:]
     scale = scale_ref[0]
     for raw, other, parts, out in (
         (img_ref, txt_hat_ref, (own_img, ring_img, sib_img), grad_img_ref),
@@ -255,7 +265,7 @@
         grad_hat = scale * (total - other[...].astype(F32))
         inner = jnp.sum(grad_hat * unit, axis=1, keepdims=True)
         out[...] = (recip * (grad_hat - unit * inner)).astype(BF16)
-    cols = col_ref[...] + decode(ring_img, 128) + decode(sib_img, 64)
+    cols = col_ref[...] + decode(for_sib, 64) + decode(sib_img, 64)
     rows = row_ref[...] + decode(txt1, 64) + decode(txt2, 64) + decode(txt3, 64)
     batch = ROWS * GROUP * GROUP
     diag_sum = scale * rows[0, 2]
@@ -294,26 +304,28 @@
     scales = jnp.stack([scale, shift])
     row_place, col_place = places()
 
+    ring1_own = ring(img_hat, 1)
+    sib = to_sibling(img_hat)
     below, above, far = first_axis(txt_hat, 1), first_axis(txt_hat, -1), first_axis(txt_hat, 2)
-    sib = to_sibling(img_hat)
-    chip = jnp.concatenate([img_hat, sib], axis=0)
-    ring1 = ring(chip, 1)
+    ring1 = jnp.concatenate([ring1_own, ring(sib, 1)], axis=0)
     line = jnp.concatenate([txt_hat, below, above, far], axis=0)
-    ring1, line = lax.optimization_barrier((ring1, line))
     up, down = second_axis(line, 1), second_axis(line, -1)
+    ring1, _ = lax.optimization_barrier((ring1, line))
     ring2 = ring(ring1, 1)
     low_far, high_far = second_axis(up[:128], 1), second_axis(down[128:], -1)
     ring3 = ring(ring2, 1)
-    ring4 = ring(ring3[:64], 1)
-    mine = [ring1, ring2, ring3, ring4]
-    img_blocks = [to_sibling(block) for block in mine] + [sib] + mine + [img_hat]
+    ring3, _, _ = lax.optimization_barrier((ring3, up, down))
+    ring4 = ring(ring3, 1)
+    img_blocks = [to_sibling(block) for block in (ring1, ring2, ring3)] + [sib, ring1, ring2, ring3, ring4, img_hat]
+    img_order = [(0, 0, 128), (1, 0, 128), (2, 0, 128), (7, 64, 64), (3, 0, 64)]
+    img_order += [(4, 0, 128), (5, 0, 128), (6, 0, 128), (7, 0, 64), (8, 0, 64)]
     txt_blocks = [line, up, down, low_far, high_far]
-    counts = [[block.shape[0] for block in blocks] for blocks in (img_blocks, txt_blocks)]
+    txt_order = [(k, 0, block.shape[0]) for k, block in enumerate(txt_blocks)]
 
     steps = total // 256
     flops = 2 * total * total * width
     img_all, txt_all, logits, row_part, col_part = call(
-        lambda *refs: logits_kernel(counts, *refs),
+        lambda *refs: logits_kernel(img_order, txt_order, *refs),
         (
             shape(total, width),
             shape(total, width),
@@ -355,10 +367,10 @@
             ],
         )(row_place, col_place, scales, logits, txt_all, *row_parts, *col_parts)
 
-    core = jnp.reshape(lax.axis_index("c"), (1,)).astype(jnp.int32)
     send, dlogits_low, row_scalars = grad_img(0)
     arrived = to_sibling(send)
     keep, dlogits_high = grad_img(1)
+    core = jnp.reshape(lax.axis_index("c"), (1,)).astype(jnp.int32)
     far, rest, own_img, col_scalars = call(
         pair_kernel,
         (shape(80, width), shape(384, width), shape(64, width), shape(8, 128, dtype=F32)),
@@ -366,46 +378,56 @@
         "pair",
     )(core, keep, arrived)
     ring1 = ring(far, -1)
-    txt_own, txt_minus, txt_plus, far_low, far_high = call(
+    far_low, far_high = call(
+        grad_txt_far_kernel,
+        (shape(144, width), shape(128, width)),
+        [VMEM] * 4,
+        "grad_txt_far",
+        flops // 4,
+    )(dlogits_low, dlogits_high, img_all, row_scalars)
+    low, high = second_axis(far_low, -1), second_axis(far_high, 1)
+    txt_own, txt_minus, txt_plus = call(
         grad_txt_kernel,
-        (shape(256, width),) * 3 + (shape(144, width), shape(128, width)),
-        [VMEM] * 4,
+        (shape(256, width),) * 3,
+        [VMEM] * 3,
         "grad_txt",
-        flops,
-        grid=(steps,),
-        out_specs=(VMEM,) * 5,
-    )(dlogits_low, dlogits_high, img_all, row_scalars)
+        flops // 4 * 3,
+        grid=(3,),
+        out_specs=(VMEM,) * 3,
+    )(dlogits_low, dlogits_high, img_all)
 
     def ring_fold(start, arrived):
         return call(
             lambda *refs: ring_fold_kernel(start, *refs), shape(144, width), [VMEM] * 3, "ring_fold"
         )(rest, arrived, col_scalars)
 
-    ring1, far_low, far_high = lax.optimization_barrier((ring1, far_low, far_high))
-    low, high = second_axis(far_low, -1), second_axis(far_high, 1)
+    ring1, _ = lax.optimization_barrier((ring1, txt_own))
     ring2 = ring(ring_fold(256, ring1), -1)
-    ring2, low, high = lax.optimization_barrier((ring2, low, high))
     to_minus, to_plus = call(
         plane_fold_kernel, (shape(272, width),) * 2, [VMEM] * 5, "plane_fold"
     )(txt_minus, txt_plus, low, high, row_scalars)
     down, up = second_axis(to_minus, -1), second_axis(to_plus, 1)
+    ring2, _ = lax.optimization_barrier((ring2, to_plus))
     ring3 = ring(ring_fold(128, ring2), -1)
-    ring3, down, up = lax.optimization_barrier((ring3, down, up))
     own_txt, *sends, row_scalars = call(
         line_kernel,
         (shape(64, width),) + (shape(80, width),) * 3 + (shape(8, 128, dtype=F32),),
         [VMEM] * 4,
         "line",
     )(txt_own, down, up, row_scalars)
-    ring4 = ring(ring_fold(0, ring3), -1)
+    ring3, _ = lax.optimization_barrier((ring3, own_txt))
+    to_own, to_sib = call(
+        last_fold_kernel, (shape(64, width), shape(80, width)), [VMEM] * 3, "last_fold"
+    )(rest, ring3, col_scalars)
+    for_sib = ring(to_sib, -1)
     txt_parts = [own_txt] + [first_axis(part, step) for part, step in zip(sends, (-1, 1, 2))]
-    img_parts = [own_img, ring4, to_sibling(ring4[64:])]
+    img_parts = [own_img, ring(to_own, -1), to_sibling(for_sib), for_sib]
 
     scalar = shape(1, dtype=F32)
     return call(
         finish_kernel,
         (shape(rows, width), shape(rows, width), scalar, scalar),
-        [SMEM] + [VMEM] * 13,
+        [SMEM] + [VMEM] * 14,
         "finish",
         out_specs=(VMEM, VMEM, SMEM, SMEM),
     )(scales, image_raw, text_raw, img_hat, txt_hat, *img_parts, *txt_parts, col_scalars, row_scalars)

time: 131 us -> 120 us (0.916)
  the two profiles are of different devices: /device:TPU:160 before, /device:TPU:1 now
where the time goes in v1:
time: 120 us
  starting transfers between devices  55.9 us (47%)
  waiting for transfers between devices  41 us (34%)
  Pallas kernels  18.4 us (15%)
  local copies, waits for them, and re-layouts  2.11 us (2%)
  between operations  1.77 us (1%)
    ppermute x41, starting transfers between devices, permute(): return lax.ppermute(array, AXES, pairs)  55.9 us
    ppermute x41, waiting for transfers between devices, permute(): return lax.ppermute(array, AXES, pairs)  41 us
    pallas_call x1, Pallas kernels, per_device(): call(lambda *refs: logits_kernel(img_order, txt_order, *refs), (shape(tot...  6.02 us
    pallas_call x2, Pallas kernels, grad_img(): call(lambda *refs: grad_img_kernel(half, *refs), (shape(total // 2 + 16,...  5.51 us
    pallas_call x1, Pallas kernels, per_device(): call(grad_txt_kernel, (shape(256, width),) * 3, [VMEM] * 3, 'grad_txt', f...  2.88 us
  transfers between devices with their start and end apart: 41, of which 16 were waited for; matrix products, arithmetic and copies ran while one was open for 1% of the time, Pallas kernels for 6%

profile of v1, /device:TPU:1, one launch (start us, length us, event | category | flops | bytes accessed | tf_op | source)
XLA Modules:
  0.0 120.0 jit_solution(16359208989605303913)
XLA Ops:
  0.7 0.9 copy-done
  1.6 0.9 copy-done.2
  2.5 0.4 normalize.1
  2.9 3.3 %collective-permute-start.1 = (bf16[64,1280]{1,0:T(8,128)(2,1)S(1)}, bf16[64,1280]{1,0:T(8,128)(2,1)S(1)}, u32[]{:S(2)}, u32[]{:S(2)}) collective-permute-start(bf16[64,1280]{1,0:T(8,128)(2,1)S(1)} %get-tuple-element.40.refs_12_.img_hat_ref), channel_id=1, source_target_pairs={{0,16},{1,17},{2,18},{3,19},{4,20},{5,21},{6,22},{7,23},{8,24},{9,... | collective-permute-start | bytes 491528 | tf_op jit(solution)/shard_map/ppermute | solution.py:44
  6.2 3.8 %collective-permute-start = (bf16[64,1280]{1,0:T(8,128)(2,1)S(1)}, bf16[64,1280]{1,0:T(8,128)(2,1)S(1)}, u32[]{:S(2)}, u32[]{:S(2)}) collective-permute-start(bf16[64,1280]{1,0:T(8,128)(2,1)S(1)} %get-tuple-element.40.refs_12_.img_hat_ref), channel_id=1, source_target_pairs={{0,1},{1,2},{2,3},{3,4},{4,5},{5,6},{6,7},{7,0},{8,9},{9,10},{10,1... | collective-permute-start | bytes 491528 | tf_op jit(solution)/shard_map/ppermute | solution.py:44
  10.0 2.9 %collective-permute-start.5 = (bf16[64,1280]{1,0:T(8,128)(2,1)S(1)}, bf16[64,1280]{1,0:T(8,128)(2,1)S(1)}, u32[]{:S(2)}, u32[]{:S(2)}) collective-permute-start(bf16[64,1280]{1,0:T(8,128)(2,1)S(1)} %get-tuple-element.41.txt_hat_ref), channel_id=1, source_target_pairs={{0,32},{1,33},{2,34},{3,35},{4,36},{5,37},{6,38},{7,39},{8,40},{9,... | collective-permute-start | bytes 491528 | tf_op jit(solution)/shard_map/ppermute | solution.py:44
  13.0 0.8 collective-permute-start.4
  13.7 0.7 collective-permute-start.3
  14.4 0.8 collective-permute-start.2
  15.2 3.9 %collective-permute-done.3 = bf16[64,1280]{1,0:T(8,128)(2,1)S(1)} collective-permute-done((bf16[64,1280]{1,0:T(8,128)(2,1)S(1)}, bf16[64,1280]{1,0:T(8,128)(2,1)S(1)}, u32[]{:S(2)}, u32[]{:S(2)}) %collective-permute-start.3) | collective-permute-done | bytes 163872 | tf_op jit(solution)/shard_map/ppermute | solution.py:44
  19.2 2.6 %collective-permute-start.11 = (bf16[256,1280]{1,0:T(8,128)(2,1)S(1)}, bf16[256,1280]{1,0:T(8,128)(2,1)S(1)}, u32[]{:S(2)}, u32[]{:S(2)}) collective-permute-start(bf16[256,1280]{1,0:T(8,128)(2,1)S(1)} %constant_dynamic-update-slice_fusion.refs_13_), channel_id=1, source_target_pairs={{0,192},{1,193},{2,194},{3,195},{4,196},{5,197},{6,198},{7,199},{8... | collective-permute-start | bytes 1966088 | tf_op jit(solution)/shard_map/ppermute | solution.py:44
  21.8 0.8 collective-permute-start.7
  22.6 5.5 %collective-permute-done.7.refs_9_ = bf16[128,1280]{1,0:T(8,128)(2,1)S(1)} collective-permute-done((bf16[128,1280]{1,0:T(8,128)(2,1)S(1)}, bf16[128,1280]{1,0:T(8,128)(2,1)S(1)}, u32[]{:S(2)}, u32[]{:S(2)}) %collective-permute-start.7) | collective-permute-done | bytes 327712 | tf_op jit(solution)/shard_map/ppermute | solution.py:44
  28.1 1.9 %collective-permute-start.9 = (bf16[128,1280]{1,0:T(8,128)(2,1)S(1)}, bf16[128,1280]{1,0:T(8,128)(2,1)S(1)}, u32[]{:S(2)}, u32[]{:S(2)}) collective-permute-start(bf16[128,1280]{1,0:T(8,128)(2,1)S(1)} %collective-permute-done.7.refs_9_), channel_id=1, source_target_pairs={{0,1},{1,2},{2,3},{3,4},{4,5},{5,6},{6,7},{7,0},{8,9},{9,10},{10,1... | collective-permute-start | bytes 983048 | tf_op jit(solution)/shard_map/ppermute | solution.py:44
  30.7 0.8 select_add_fusion
  31.7 0.5 collective-permute-start.8
  32.3 2.7 %collective-permute-start.15 = (bf16[128,1280]{1,0:T(8,128)(2,1)S(1)}, bf16[128,1280]{1,0:T(8,128)(2,1)S(1)}, u32[]{:S(2)}, u32[]{:S(2)}) collective-permute-start(bf16[128,1280]{1,0:T(8,128)(2,1)S(1)} %slice.9), channel_id=1, source_target_pairs={{0,192},{1,193},{2,194},{3,195},{4,196},{5,197},{6,198},{7,199},{8... | collective-permute-start | bytes 983048 | tf_op jit(solution)/shard_map/ppermute | solution.py:44
  35.1 2.0 %collective-permute-start.13 = (bf16[128,1280]{1,0:T(8,128)(2,1)S(1)}, bf16[128,1280]{1,0:T(8,128)(2,1)S(1)}, u32[]{:S(2)}, u32[]{:S(2)}) collective-permute-start(bf16[128,1280]{1,0:T(8,128)(2,1)S(1)} %collective-permute-done.9.refs_10_), channel_id=1, source_target_pairs={{0,1},{1,2},{2,3},{3,4},{4,5},{5,6},{6,7},{7,0},{8,9},{9,10},{10,1... | collective-permute-start | bytes 983048 | tf_op jit(solution)/shard_map/ppermute | solution.py:44
  37.2 0.7 collective-permute-start.12
  37.9 1.1 collective-permute-done.15.refs_17_
  39.0 3.5 %collective-permute-done.14.refs_16_ = bf16[128,1280]{1,0:T(8,128)(2,1)S(1)} collective-permute-done((bf16[128,1280]{1,0:T(8,128)(2,1)S(1)}, bf16[128,1280]{1,0:T(8,128)(2,1)S(1)}, u32[]{:S(2)}, u32[]{:S(2)}) %collective-permute-start.14) | collective-permute-done | bytes 327712 | tf_op jit(solution)/shard_map/ppermute | solution.py:44
  42.5 6.0 %logits.1 = (bf16[1024,1280]{1,0:T(8,128)(2,1)S(1)}, bf16[1024,1280]{1,0:T(8,128)(2,1)S(1)}, f32[1024,1024]{1,0:T(8,128)S(1)}, f32[24,128]{1,0:T(8,128)S(1)}, f32[16,128]{1,0:T(8,128)S(1)}) custom-call(s32[16]{0:T(128)S(1)} %get-tuple-element.80.refs_0_, s32[16]{0:T(128)S(1)} %get-tuple-element.81.refs_1_, f32[2]{0:T(128)S(1)} %pad_maximum_fusion.1.refs_2_.scale_ref, ...), custom_call_target="tpu_custom_call" | custom-call | flops 2684354560 | bytes 1048576 | tf_op jit(solution)/shard_map/logits/pallas_call | solution.py:327
  48.6 3.6 %collective-permute-start.16 = (f32[24,128]{1,0:T(8,128)S(1)}, f32[24,128]{1,0:T(8,128)S(1)}, u32[]{:S(2)}, u32[]{:S(2)}) collective-permute-start(f32[24,128]{1,0:T(8,128)S(1)} %get-tuple-element.47), channel_id=1, source_target_pairs={{0,16},{1,17},{2,18},{3,19},{4,20},{5,21},{6,22},{7,23},{8,24},{9,... | collective-permute-start | bytes 36872 | tf_op jit(solution)/shard_map/ppermute | solution.py:44
  52.2 0.8 collective-permute-done.16
  53.0 0.3 collective-permute-start.18
  53.4 1.1 collective-permute-start.17
  54.5 0.3 collective-permute-start.23
  54.8 0.9 collective-permute-start.22
  55.7 0.3 collective-permute-start.21
  56.0 1.1 collective-permute-done.17
  57.2 3.9 %collective-permute-start.20 = (f32[24,128]{1,0:T(8,128)S(1)}, f32[24,128]{1,0:T(8,128)S(1)}, u32[]{:S(2)}, u32[]{:S(2)}) collective-permute-start(f32[24,128]{1,0:T(8,128)S(1)} %get-tuple-element.77), channel_id=1, source_target_pairs={{0,5},{1,6},{2,7},{3,0},{4,1},{5,2},{6,3},{7,4},{8,13},{9,14},{10,... | collective-permute-start | bytes 36872 | tf_op jit(solution)/shard_map/ppermute | solution.py:44
  61.1 3.0 %collective-permute-start.26 = (f32[16,128]{1,0:T(8,128)S(1)}, f32[16,128]{1,0:T(8,128)S(1)}, u32[]{:S(2)}, u32[]{:S(2)}) collective-permute-start(f32[16,128]{1,0:T(8,128)S(1)} %add_add_fusion.refs_8_), channel_id=1, source_target_pairs={{0,192},{1,193},{2,194},{3,195},{4,196},{5,197},{6,198},{7,199},{8... | collective-permute-start | bytes 24584 | tf_op jit(solution)/shard_map/ppermute | solution.py:44
  64.1 0.7 collective-permute-start.24
  64.8 0.1 collective-permute-done.26.refs_11_
  64.9 3.2 %collective-permute-done.25.refs_10_ = f32[16,128]{1,0:T(8,128)S(1)} collective-permute-done((f32[16,128]{1,0:T(8,128)S(1)}, f32[16,128]{1,0:T(8,128)S(1)}, u32[]{:S(2)}, u32[]{:S(2)}) %collective-permute-start.25) | collective-permute-done | bytes 8224 | tf_op jit(solution)/shard_map/ppermute | solution.py:44
  68.2 2.8 %grad_img0.1 = (bf16[528,1280]{1,0:T(8,128)(2,1)S(1)}, bf16[512,1024]{1,0:T(8,128)(2,1)S(1)}, f32[8,128]{1,0:T(8,128)S(1)}) custom-call(s32[16]{0:T(128)S(1)} %get-tuple-element.80.refs_0_, s32[16]{0:T(128)S(1)} %get-tuple-element.81.refs_1_, f32[2]{0:T(128)S(1)} %pad_maximum_fusion.1.refs_2_.scale_ref, f32[1024,1024]{1,0:T(8,128)S(1)} %get-tuple-element.45.refs_3_, ...), custom_call_target="tpu_custom_call" | custom-call | flops 1342177280 | bytes 1048576 | tf_op jit(solution)/shard_map/grad_img0/pallas_call | solution.py:354
  70.9 3.8 %collective-permute-start.27 = (bf16[528,1280]{1,0:T(8,128)(2,1)S(1)}, bf16[528,1280]{1,0:T(8,128)(2,1)S(1)}, u32[]{:S(2)}, u32[]{:S(2)}) collective-permute-start(bf16[528,1280]{1,0:T(8,128)(2,1)S(1)} %get-tuple-element.50), channel_id=1, source_target_pairs={{0,16},{1,17},{2,18},{3,19},{4,20},{5,21},{6,22},{7,23},{8,24},{9,... | collective-permute-start | bytes 4055048 | tf_op jit(solution)/shard_map/ppermute | solution.py:44
  74.7 2.7 %grad_img1.1 = (bf16[528,1280]{1,0:T(8,128)(2,1)S(1)}, bf16[512,1024]{1,0:T(8,128)(2,1)S(1)}) custom-call(s32[16]{0:T(128)S(1)} %get-tuple-element.80.refs_0_, s32[16]{0:T(128)S(1)} %get-tuple-element.81.refs_1_, f32[2]{0:T(128)S(1)} %pad_maximum_fusion.1.refs_2_.scale_ref, f32[1024,1024]{1,0:T(8,128)S(1)} %get-tuple-element.45.refs_3_, ...), custom_call_target="tpu_custom_call" | custom-call | flops 1342177280 | bytes 1048576 | tf_op jit(solution)/shard_map/grad_img1/pallas_call | solution.py:354
  77.5 0.9 grad_txt_far.1
  78.4 1.3 %collective-permute-start.30 = (bf16[144,1280]{1,0:T(8,128)(2,1)S(1)}, bf16[144,1280]{1,0:T(8,128)(2,1)S(1)}, u32[]{:S(2)}, u32[]{:S(2)}) collective-permute-start(bf16[144,1280]{1,0:T(8,128)(2,1)S(1)} %get-tuple-element.63), channel_id=1, source_target_pairs={{0,192},{1,193},{2,194},{3,195},{4,196},{5,197},{6,198},{7,199},{8... | collective-permute-start | bytes 1105928 | tf_op jit(solution)/shard_map/ppermute | solution.py:44
  79.6 0.3 collective-permute-start.31
  79.9 0.3 pair.1
  80.2 1.5 %collective-permute-start.28 = (bf16[80,1280]{1,0:T(8,128)(2,1)S(1)}, bf16[80,1280]{1,0:T(8,128)(2,1)S(1)}, u32[]{:S(2)}, u32[]{:S(2)}) collective-permute-start(bf16[80,1280]{1,0:T(8,128)(2,1)S(1)} %get-tuple-element.53), channel_id=1, source_target_pairs={{0,7},{1,0},{2,1},{3,2},{4,3},{5,4},{6,5},{7,6},{8,15},{9,8},{10,9... | collective-permute-start | bytes 614408 | tf_op jit(solution)/shard_map/ppermute | solution.py:44
  81.8 2.9 %grad_txt.1 = (bf16[256,1280]{1,0:T(8,128)(2,1)S(1)}, bf16[256,1280]{1,0:T(8,128)(2,1)S(1)}, bf16[256,1280]{1,0:T(8,128)(2,1)S(1)}) custom-call(bf16[512,1024]{1,0:T(8,128)(2,1)S(1)} %get-tuple-element.54.low_ref, bf16[512,1024]{1,0:T(8,128)(2,1)S(1)} %get-tuple-element.55.high_ref, bf16[1024,1280]{1,0:T(8,128)(2,1)S(1)} %get-tuple-element.56.img_ref), custom_call_target="tpu_custom_call" | custom-call | flops 2013265920 | bytes 1048576 | tf_op jit(solution)/shard_map/grad_txt/pallas_call | solution.py:389
  84.7 1.8 %collective-permute-done.28.refs_1_ = bf16[80,1280]{1,0:T(8,128)(2,1)S(1)} collective-permute-done((bf16[80,1280]{1,0:T(8,128)(2,1)S(1)}, bf16[80,1280]{1,0:T(8,128)(2,1)S(1)}, u32[]{:S(2)}, u32[]{:S(2)}) %collective-permute-start.28) | collective-permute-done | bytes 204832 | tf_op jit(solution)/shard_map/ppermute | solution.py:44
  86.5 0.3 collective-permute-start.29
  86.8 0.2 collective-permute-done.31.high_ref
  87.1 0.2 plane_fold.1
  87.3 2.5 %collective-permute-start.33 = (bf16[272,1280]{1,0:T(8,128)(2,1)S(1)}, bf16[272,1280]{1,0:T(8,128)(2,1)S(1)}, u32[]{:S(2)}, u32[]{:S(2)}) collective-permute-start(bf16[272,1280]{1,0:T(8,128)(2,1)S(1)} %get-tuple-element.67), channel_id=1, source_target_pairs={{0,192},{1,193},{2,194},{3,195},{4,196},{5,197},{6,198},{7,199},{8... | collective-permute-start | bytes 2088968 | tf_op jit(solution)/shard_map/ppermute | solution.py:44
  89.8 4.3 %collective-permute-done.29.refs_1_ = bf16[144,1280]{1,0:T(8,128)(2,1)S(1)} collective-permute-done((bf16[144,1280]{1,0:T(8,128)(2,1)S(1)}, bf16[144,1280]{1,0:T(8,128)(2,1)S(1)}, u32[]{:S(2)}, u32[]{:S(2)}) %collective-permute-start.29) | collective-permute-done | bytes 368672 | tf_op jit(solution)/shard_map/ppermute | solution.py:44
  94.2 0.1 ring_fold.3
  94.3 3.4 %collective-permute-done.33.down_ref = bf16[272,1280]{1,0:T(8,128)(2,1)S(1)} collective-permute-done((bf16[272,1280]{1,0:T(8,128)(2,1)S(1)}, bf16[272,1280]{1,0:T(8,128)(2,1)S(1)}, u32[]{:S(2)}, u32[]{:S(2)}) %collective-permute-start.33) | collective-permute-done | bytes 696352 | tf_op jit(solution)/shard_map/ppermute | solution.py:44
  97.8 3.4 %collective-permute-done.34.up_ref = bf16[272,1280]{1,0:T(8,128)(2,1)S(1)} collective-permute-done((bf16[272,1280]{1,0:T(8,128)(2,1)S(1)}, bf16[272,1280]{1,0:T(8,128)(2,1)S(1)}, u32[]{:S(2)}, u32[]{:S(2)}) %collective-permute-start.34) | collective-permute-done | bytes 696352 | tf_op jit(solution)/shard_map/ppermute | solution.py:44
  101.2 0.2 line.1
  101.4 0.8 collective-permute-done.32.arrived_ref
  102.2 0.1 last_fold.1
  102.3 0.8 collective-permute-start.36
  103.1 0.5 collective-permute-start.38
  103.6 1.0 collective-permute-start.39
  104.6 1.4 %collective-permute-start.40 = (bf16[80,1280]{1,0:T(8,128)(2,1)S(1)}, bf16[80,1280]{1,0:T(8,128)(2,1)S(1)}, u32[]{:S(2)}, u32[]{:S(2)}) collective-permute-start(bf16[80,1280]{1,0:T(8,128)(2,1)S(1)} %get-tuple-element.74), channel_id=1, source_target_pairs={{0,32},{1,33},{2,34},{3,35},{4,36},{5,37},{6,38},{7,39},{8,40},{9,... | collective-permute-start | bytes 614408 | tf_op jit(solution)/shard_map/ppermute | solution.py:44
  106.0 2.2 %collective-permute-done.36.refs_3_ = bf16[80,1280]{1,0:T(8,128)(2,1)S(1)} collective-permute-done((bf16[80,1280]{1,0:T(8,128)(2,1)S(1)}, bf16[80,1280]{1,0:T(8,128)(2,1)S(1)}, u32[]{:S(2)}, u32[]{:S(2)}) %collective-permute-start.36) | collective-permute-done | bytes 204832 | tf_op jit(solution)/shard_map/ppermute | solution.py:44
  108.2 4.4 %collective-permute-start.37 = (bf16[80,1280]{1,0:T(8,128)(2,1)S(1)}, bf16[80,1280]{1,0:T(8,128)(2,1)S(1)}, u32[]{:S(2)}, u32[]{:S(2)}) collective-permute-start(bf16[80,1280]{1,0:T(8,128)(2,1)S(1)} %collective-permute-done.36.refs_3_), channel_id=1, source_target_pairs={{0,16},{1,17},{2,18},{3,19},{4,20},{5,21},{6,22},{7,23},{8,24},{9,... | collective-permute-start | bytes 614408 | tf_op jit(solution)/shard_map/ppermute | solution.py:44
  112.6 5.5 %collective-permute-done.35.refs_1_ = bf16[64,1280]{1,0:T(8,128)(2,1)S(1)} collective-permute-done((bf16[64,1280]{1,0:T(8,128)(2,1)S(1)}, bf16[64,1280]{1,0:T(8,128)(2,1)S(1)}, u32[]{:S(2)}, u32[]{:S(2)}) %collective-permute-start.35) | collective-permute-done | bytes 163872 | tf_op jit(solution)/shard_map/ppermute | solution.py:44
  118.2 1.7 %finish.1 = (bf16[64,1280]{1,0:T(8,128)(2,1)}, bf16[64,1280]{1,0:T(8,128)(2,1)}, f32[1]{0:T(128)}, f32[1]{0:T(128)}) custom-call(f32[2]{0:T(128)S(1)} %pad_maximum_fusion.1.refs_2_.scale_ref, bf16[64,1280]{1,0:T(8,128)(2,1)S(1)} %copy-done.1, bf16[64,1280]{1,0:T(8,128)(2,1)S(1)} %copy-done.3, bf16[64,1280]{1,0:T(8,128)(2,1)S(1)} %get-tuple-element.40.refs_12_.img_hat_ref, ...), custom_call_target="tpu_custom_call" | custom-call | bytes 1048576 | tf_op jit(solution)/shard_map/finish/pallas_call | solution.py:427
  (58 shorter events, 0.7 us)
Async XLA Ops:
  0.6 37.3 %copy-start.4 = (s32[16]{0:T(128)S(1)}, s32[16]{0:T(128)}, u32[]{:S(2)}) copy-start(s32[16]{0:T(128)} %constant.88.clone) | copy-start | bytes 196
  0.6 0.9 copy-start
  1.6 0.9 copy-start.2
  2.5 35.4 %copy-start.5 = (s32[16]{0:T(128)S(1)}, s32[16]{0:T(128)}, u32[]{:S(2)}) copy-start(s32[16]{0:T(128)} %constant.87.clone) | copy-start | bytes 196
  2.9 11.6 %collective-permute-start.1 = (bf16[64,1280]{1,0:T(8,128)(2,1)S(1)}, bf16[64,1280]{1,0:T(8,128)(2,1)S(1)}, u32[]{:S(2)}, u32[]{:S(2)}) collective-permute-start(bf16[64,1280]{1,0:T(8,128)(2,1)S(1)} %get-tuple-element.40.refs_12_.img_hat_ref), channel_id=1, source_target_pairs={{0,16},{1,17},{2,18},{3,19},{4,20},{5,21},{6,22},{7,23},{8,24},{9,... | collective-permute-start | bytes 491528 | tf_op jit(solution)/shard_map/ppermute | solution.py:44
  6.2 15.6 %collective-permute-start = (bf16[64,1280]{1,0:T(8,128)(2,1)S(1)}, bf16[64,1280]{1,0:T(8,128)(2,1)S(1)}, u32[]{:S(2)}, u32[]{:S(2)}) collective-permute-start(bf16[64,1280]{1,0:T(8,128)(2,1)S(1)} %get-tuple-element.40.refs_12_.img_hat_ref), channel_id=1, source_target_pairs={{0,1},{1,2},{2,3},{3,4},{4,5},{5,6},{6,7},{7,0},{8,9},{9,10},{10,1... | collective-permute-start | bytes 491528 | tf_op jit(solution)/shard_map/ppermute | solution.py:44
  10.0 9.1 %collective-permute-start.5 = (bf16[64,1280]{1,0:T(8,128)(2,1)S(1)}, bf16[64,1280]{1,0:T(8,128)(2,1)S(1)}, u32[]{:S(2)}, u32[]{:S(2)}) collective-permute-start(bf16[64,1280]{1,0:T(8,128)(2,1)S(1)} %get-tuple-element.41.txt_hat_ref), channel_id=1, source_target_pairs={{0,32},{1,33},{2,34},{3,35},{4,36},{5,37},{6,38},{7,39},{8,40},{9,... | collective-permute-start | bytes 491528 | tf_op jit(solution)/shard_map/ppermute | solution.py:44
  13.0 6.2 %collective-permute-start.4 = (bf16[64,1280]{1,0:T(8,128)(2,1)S(1)}, bf16[64,1280]{1,0:T(8,128)(2,1)S(1)}, u32[]{:S(2)}, u32[]{:S(2)}) collective-permute-start(bf16[64,1280]{1,0:T(8,128)(2,1)S(1)} %get-tuple-element.41.txt_hat_ref), channel_id=1, source_target_pairs={{0,40},{1,41},{2,42},{3,43},{4,44},{5,45},{6,46},{7,47},{8,0},{9,1... | collective-permute-start | bytes 491528 | tf_op jit(solution)/shard_map/ppermute | solution.py:44
  13.7 5.4 %collective-permute-start.3 = (bf16[64,1280]{1,0:T(8,128)(2,1)S(1)}, bf16[64,1280]{1,0:T(8,128)(2,1)S(1)}, u32[]{:S(2)}, u32[]{:S(2)}) collective-permute-start(bf16[64,1280]{1,0:T(8,128)(2,1)S(1)} %get-tuple-element.41.txt_hat_ref), channel_id=1, source_target_pairs={{0,8},{1,9},{2,10},{3,11},{4,12},{5,13},{6,14},{7,15},{8,32},{9,33... | collective-permute-start | bytes 491528 | tf_op jit(solution)/shard_map/ppermute | solution.py:44
  14.4 7.3 %collective-permute-start.2 = (bf16[64,1280]{1,0:T(8,128)(2,1)S(1)}, bf16[64,1280]{1,0:T(8,128)(2,1)S(1)}, u32[]{:S(2)}, u32[]{:S(2)}) collective-permute-start(bf16[64,1280]{1,0:T(8,128)(2,1)S(1)} %collective-permute-done.1.refs_7_), channel_id=1, source_target_pairs={{0,1},{1,2},{2,3},{3,4},{4,5},{5,6},{6,7},{7,0},{8,9},{9,10},{10,1... | collective-permute-start | bytes 491528 | tf_op jit(solution)/shard_map/ppermute | solution.py:44
  19.2 13.0 %collective-permute-start.11 = (bf16[256,1280]{1,0:T(8,128)(2,1)S(1)}, bf16[256,1280]{1,0:T(8,128)(2,1)S(1)}, u32[]{:S(2)}, u32[]{:S(2)}) collective-permute-start(bf16[256,1280]{1,0:T(8,128)(2,1)S(1)} %constant_dynamic-update-slice_fusion.refs_13_), channel_id=1, source_target_pairs={{0,192},{1,193},{2,194},{3,195},{4,196},{5,197},{6,198},{7,199},{8... | collective-permute-start | bytes 1966088 | tf_op jit(solution)/shard_map/ppermute | solution.py:44
  21.7 13.3 %collective-permute-start.10 = (bf16[256,1280]{1,0:T(8,128)(2,1)S(1)}, bf16[256,1280]{1,0:T(8,128)(2,1)S(1)}, u32[]{:S(2)}, u32[]{:S(2)}) collective-permute-start(bf16[256,1280]{1,0:T(8,128)(2,1)S(1)} %constant_dynamic-update-slice_fusion.refs_13_), channel_id=1, source_target_pairs={{0,64},{1,65},{2,66},{3,67},{4,68},{5,69},{6,70},{7,71},{8,72},{9,... | collective-permute-start | bytes 1966088 | tf_op jit(solution)/shard_map/ppermute | solution.py:44
  21.8 6.3 %collective-permute-start.7 = (bf16[128,1280]{1,0:T(8,128)(2,1)S(1)}, bf16[128,1280]{1,0:T(8,128)(2,1)S(1)}, u32[]{:S(2)}, u32[]{:S(2)}) collective-permute-start(bf16[128,1280]{1,0:T(8,128)(2,1)S(1)} %pad_maximum_fusion.refs_8_), channel_id=1, source_target_pairs={{0,1},{1,2},{2,3},{3,4},{4,5},{5,6},{6,7},{7,0},{8,9},{9,10},{10,1... | collective-permute-start | bytes 983048 | tf_op jit(solution)/shard_map/ppermute | solution.py:44
  28.1 7.0 %collective-permute-start.9 = (bf16[128,1280]{1,0:T(8,128)(2,1)S(1)}, bf16[128,1280]{1,0:T(8,128)(2,1)S(1)}, u32[]{:S(2)}, u32[]{:S(2)}) collective-permute-start(bf16[128,1280]{1,0:T(8,128)(2,1)S(1)} %collective-permute-done.7.refs_9_), channel_id=1, source_target_pairs={{0,1},{1,2},{2,3},{3,4},{4,5},{5,6},{6,7},{7,0},{8,9},{9,10},{10,1... | collective-permute-start | bytes 983048 | tf_op jit(solution)/shard_map/ppermute | solution.py:44
  30.0 7.1 %collective-permute-start.6 = (bf16[128,1280]{1,0:T(8,128)(2,1)S(1)}, bf16[128,1280]{1,0:T(8,128)(2,1)}, u32[]{:S(2)}, u32[]{:S(2)}) collective-permute-start(bf16[128,1280]{1,0:T(8,128)(2,1)S(1)} %pad_maximum_fusion.refs_8_), channel_id=1, source_target_pairs={{0,16},{1,17},{2,18},{3,19},{4,20},{5,21},{6,22},{7,23},{8,24},{9,... | collective-permute-start | bytes 983048 | tf_op jit(solution)/shard_map/ppermute | solution.py:44
  31.7 6.2 %collective-permute-start.8 = (bf16[128,1280]{1,0:T(8,128)(2,1)S(1)}, bf16[128,1280]{1,0:T(8,128)(2,1)S(1)}, u32[]{:S(2)}, u32[]{:S(2)}) collective-permute-start(bf16[128,1280]{1,0:T(8,128)(2,1)S(1)} %collective-permute-done.7.refs_9_), channel_id=1, source_target_pairs={{0,16},{1,17},{2,18},{3,19},{4,20},{5,21},{6,22},{7,23},{8,24},{9,... | collective-permute-start | bytes 983048 | tf_op jit(solution)/shard_map/ppermute | solution.py:44
  32.3 6.8 %collective-permute-start.15 = (bf16[128,1280]{1,0:T(8,128)(2,1)S(1)}, bf16[128,1280]{1,0:T(8,128)(2,1)S(1)}, u32[]{:S(2)}, u32[]{:S(2)}) collective-permute-start(bf16[128,1280]{1,0:T(8,128)(2,1)S(1)} %slice.9), channel_id=1, source_target_pairs={{0,192},{1,193},{2,194},{3,195},{4,196},{5,197},{6,198},{7,199},{8... | collective-permute-start | bytes 983048 | tf_op jit(solution)/shard_map/ppermute | solution.py:44
  35.0 7.5 %collective-permute-start.14 = (bf16[128,1280]{1,0:T(8,128)(2,1)S(1)}, bf16[128,1280]{1,0:T(8,128)(2,1)S(1)}, u32[]{:S(2)}, u32[]{:S(2)}) collective-permute-start(bf16[128,1280]{1,0:T(8,128)(2,1)S(1)} %slice.8), channel_id=1, source_target_pairs={{0,64},{1,65},{2,66},{3,67},{4,68},{5,69},{6,70},{7,71},{8,72},{9,... | collective-permute-start | bytes 983048 | tf_op jit(solution)/shard_map/ppermute | solution.py:44
  35.1 7.4 %collective-permute-start.13 = (bf16[128,1280]{1,0:T(8,128)(2,1)S(1)}, bf16[128,1280]{1,0:T(8,128)(2,1)S(1)}, u32[]{:S(2)}, u32[]{:S(2)}) collective-permute-start(bf16[128,1280]{1,0:T(8,128)(2,1)S(1)} %collective-permute-done.9.refs_10_), channel_id=1, source_target_pairs={{0,1},{1,2},{2,3},{3,4},{4,5},{5,6},{6,7},{7,0},{8,9},{9,10},{10,1... | collective-permute-start | bytes 983048 | tf_op jit(solution)/shard_map/ppermute | solution.py:44
  37.2 5.4 %collective-permute-start.12 = (bf16[128,1280]{1,0:T(8,128)(2,1)S(1)}, bf16[128,1280]{1,0:T(8,128)(2,1)S(1)}, u32[]{:S(2)}, u32[]{:S(2)}) collective-permute-start(bf16[128,1280]{1,0:T(8,128)(2,1)S(1)} %collective-permute-done.9.refs_10_), channel_id=1, source_target_pairs={{0,16},{1,17},{2,18},{3,19},{4,20},{5,21},{6,22},{7,23},{8,24},{9,... | collective-permute-start | bytes 983048 | tf_op jit(solution)/shard_map/ppermute | solution.py:44
  48.6 4.5 %collective-permute-start.16 = (f32[24,128]{1,0:T(8,128)S(1)}, f32[24,128]{1,0:T(8,128)S(1)}, u32[]{:S(2)}, u32[]{:S(2)}) collective-permute-start(f32[24,128]{1,0:T(8,128)S(1)} %get-tuple-element.47), channel_id=1, source_target_pairs={{0,16},{1,17},{2,18},{3,19},{4,20},{5,21},{6,22},{7,23},{8,24},{9,... | collective-permute-start | bytes 36872 | tf_op jit(solution)/shard_map/ppermute | solution.py:44
  53.0 3.0 %collective-permute-start.18 = (f32[24,128]{1,0:T(8,128)S(1)}, f32[24,128]{1,0:T(8,128)S(1)}, u32[]{:S(2)}, u32[]{:S(2)}) collective-permute-start(f32[24,128]{1,0:T(8,128)S(1)} %add.94), channel_id=1, source_target_pairs={{0,7},{1,0},{2,1},{3,2},{4,3},{5,4},{6,5},{7,6},{8,15},{9,8},{10,9... | collective-permute-start | bytes 36872 | tf_op jit(solution)/shard_map/ppermute | solution.py:44
  53.4 3.8 %collective-permute-start.17 = (f32[24,128]{1,0:T(8,128)S(1)}, f32[24,128]{1,0:T(8,128)S(1)}, u32[]{:S(2)}, u32[]{:S(2)}) collective-permute-start(f32[24,128]{1,0:T(8,128)S(1)} %add.94), channel_id=1, source_target_pairs={{0,1},{1,2},{2,3},{3,4},{4,5},{5,6},{6,7},{7,0},{8,9},{9,10},{10,1... | collective-permute-start | bytes 36872 | tf_op jit(solution)/shard_map/ppermute | solution.py:44
  54.5 6.6 %collective-permute-start.23 = (f32[16,128]{1,0:T(8,128)S(1)}, f32[16,128]{1,0:T(8,128)S(1)}, u32[]{:S(2)}, u32[]{:S(2)}) collective-permute-start(f32[16,128]{1,0:T(8,128)S(1)} %get-tuple-element.48), channel_id=1, source_target_pairs={{0,40},{1,41},{2,42},{3,43},{4,44},{5,45},{6,46},{7,47},{8,0},{9,1... | collective-permute-start | bytes 24584 | tf_op jit(solution)/shard_map/ppermute | solution.py:44
  54.8 6.3 %collective-permute-start.22 = (f32[16,128]{1,0:T(8,128)S(1)}, f32[16,128]{1,0:T(8,128)S(1)}, u32[]{:S(2)}, u32[]{:S(2)}) collective-permute-start(f32[16,128]{1,0:T(8,128)S(1)} %get-tuple-element.48), channel_id=1, source_target_pairs={{0,32},{1,33},{2,34},{3,35},{4,36},{5,37},{6,38},{7,39},{8,40},{9,... | collective-permute-start | bytes 24584 | tf_op jit(solution)/shard_map/ppermute | solution.py:44
  55.7 5.4 %collective-permute-start.21 = (f32[16,128]{1,0:T(8,128)S(1)}, f32[16,128]{1,0:T(8,128)S(1)}, u32[]{:S(2)}, u32[]{:S(2)}) collective-permute-start(f32[16,128]{1,0:T(8,128)S(1)} %get-tuple-element.48), channel_id=1, source_target_pairs={{0,8},{1,9},{2,10},{3,11},{4,12},{5,13},{6,14},{7,15},{8,32},{9,33... | collective-permute-start | bytes 24584 | tf_op jit(solution)/shard_map/ppermute | solution.py:44
  57.2 11.0 %collective-permute-start.20 = (f32[24,128]{1,0:T(8,128)S(1)}, f32[24,128]{1,0:T(8,128)S(1)}, u32[]{:S(2)}, u32[]{:S(2)}) collective-permute-start(f32[24,128]{1,0:T(8,128)S(1)} %get-tuple-element.77), channel_id=1, source_target_pairs={{0,5},{1,6},{2,7},{3,0},{4,1},{5,2},{6,3},{7,4},{8,13},{9,14},{10,... | collective-permute-start | bytes 36872 | tf_op jit(solution)/shard_map/ppermute | solution.py:44
  61.1 7.1 %collective-permute-start.19 = (f32[24,128]{1,0:T(8,128)S(1)}, f32[24,128]{1,0:T(8,128)S(1)}, u32[]{:S(2)}, u32[]{:S(2)}) collective-permute-start(f32[24,128]{1,0:T(8,128)S(1)} %get-tuple-element.76.refs_5_), channel_id=1, source_target_pairs={{0,3},{1,4},{2,5},{3,6},{4,7},{5,0},{6,1},{7,2},{8,11},{9,12},{10,... | collective-permute-start | bytes 36872 | tf_op jit(solution)/shard_map/ppermute | solution.py:44
  61.1 3.8 %collective-permute-start.26 = (f32[16,128]{1,0:T(8,128)S(1)}, f32[16,128]{1,0:T(8,128)S(1)}, u32[]{:S(2)}, u32[]{:S(2)}) collective-permute-start(f32[16,128]{1,0:T(8,128)S(1)} %add_add_fusion.refs_8_), channel_id=1, source_target_pairs={{0,192},{1,193},{2,194},{3,195},{4,196},{5,197},{6,198},{7,199},{8... | collective-permute-start | bytes 24584 | tf_op jit(solution)/shard_map/ppermute | solution.py:44
  64.1 4.0 %collective-permute-start.25 = (f32[16,128]{1,0:T(8,128)S(1)}, f32[16,128]{1,0:T(8,128)S(1)}, u32[]{:S(2)}, u32[]{:S(2)}) collective-permute-start(f32[16,128]{1,0:T(8,128)S(1)} %add_add_fusion.refs_8_), channel_id=1, source_target_pairs={{0,128},{1,129},{2,130},{3,131},{4,132},{5,133},{6,134},{7,135},{8... | collective-permute-start | bytes 24584 | tf_op jit(solution)/shard_map/ppermute | solution.py:44
  64.1 4.0 %collective-permute-start.24 = (f32[16,128]{1,0:T(8,128)S(1)}, f32[16,128]{1,0:T(8,128)S(1)}, u32[]{:S(2)}, u32[]{:S(2)}) collective-permute-start(f32[16,128]{1,0:T(8,128)S(1)} %add_add_fusion.refs_8_), channel_id=1, source_target_pairs={{0,64},{1,65},{2,66},{3,67},{4,68},{5,69},{6,70},{7,71},{8,72},{9,... | collective-permute-start | bytes 24584 | tf_op jit(solution)/shard_map/ppermute | solution.py:44
  70.9 9.0 %collective-permute-start.27 = (bf16[528,1280]{1,0:T(8,128)(2,1)S(1)}, bf16[528,1280]{1,0:T(8,128)(2,1)S(1)}, u32[]{:S(2)}, u32[]{:S(2)}) collective-permute-start(bf16[528,1280]{1,0:T(8,128)(2,1)S(1)} %get-tuple-element.50), channel_id=1, source_target_pairs={{0,16},{1,17},{2,18},{3,19},{4,20},{5,21},{6,22},{7,23},{8,24},{9,... | collective-permute-start | bytes 4055048 | tf_op jit(solution)/shard_map/ppermute | solution.py:44
  78.4 8.7 %collective-permute-start.30 = (bf16[144,1280]{1,0:T(8,128)(2,1)S(1)}, bf16[144,1280]{1,0:T(8,128)(2,1)S(1)}, u32[]{:S(2)}, u32[]{:S(2)}) collective-permute-start(bf16[144,1280]{1,0:T(8,128)(2,1)S(1)} %get-tuple-element.63), channel_id=1, source_target_pairs={{0,192},{1,193},{2,194},{3,195},{4,196},{5,197},{6,198},{7,199},{8... | collective-permute-start | bytes 1105928 | tf_op jit(solution)/shard_map/ppermute | solution.py:44
  79.6 7.4 %collective-permute-start.31 = (bf16[128,1280]{1,0:T(8,128)(2,1)S(1)}, bf16[128,1280]{1,0:T(8,128)(2,1)S(1)}, u32[]{:S(2)}, u32[]{:S(2)}) collective-permute-start(bf16[128,1280]{1,0:T(8,128)(2,1)S(1)} %get-tuple-element.64), channel_id=1, source_target_pairs={{0,64},{1,65},{2,66},{3,67},{4,68},{5,69},{6,70},{7,71},{8,72},{9,... | collective-permute-start | bytes 983048 | tf_op jit(solution)/shard_map/ppermute | solution.py:44
  80.2 6.2 %collective-permute-start.28 = (bf16[80,1280]{1,0:T(8,128)(2,1)S(1)}, bf16[80,1280]{1,0:T(8,128)(2,1)S(1)}, u32[]{:S(2)}, u32[]{:S(2)}) collective-permute-start(bf16[80,1280]{1,0:T(8,128)(2,1)S(1)} %get-tuple-element.53), channel_id=1, source_target_pairs={{0,7},{1,0},{2,1},{3,2},{4,3},{5,4},{6,5},{7,6},{8,15},{9,8},{10,9... | collective-permute-start | bytes 614408 | tf_op jit(solution)/shard_map/ppermute | solution.py:44
  86.5 7.6 %collective-permute-start.29 = (bf16[144,1280]{1,0:T(8,128)(2,1)S(1)}, bf16[144,1280]{1,0:T(8,128)(2,1)S(1)}, u32[]{:S(2)}, u32[]{:S(2)}) collective-permute-start(bf16[144,1280]{1,0:T(8,128)(2,1)S(1)} %ring_fold.2), channel_id=1, source_target_pairs={{0,7},{1,0},{2,1},{3,2},{4,3},{5,4},{6,5},{7,6},{8,15},{9,8},{10,9... | collective-permute-start | bytes 1105928 | tf_op jit(solution)/shard_map/ppermute | solution.py:44
  87.3 30.9 %copy-start.1 = (bf16[64,1280]{1,0:T(8,128)(2,1)S(1)}, bf16[64,1280]{1,0:T(8,128)(2,1)}, u32[]{:S(2)}) copy-start(bf16[64,1280]{1,0:T(8,128)(2,1)} %img_ref.3) | copy-start | bytes 491524
  87.3 30.9 %copy-start.3 = (bf16[64,1280]{1,0:T(8,128)(2,1)S(1)}, bf16[64,1280]{1,0:T(8,128)(2,1)}, u32[]{:S(2)}) copy-start(bf16[64,1280]{1,0:T(8,128)(2,1)} %txt_ref.3) | copy-start | bytes 491524
  87.3 10.5 %collective-permute-start.33 = (bf16[272,1280]{1,0:T(8,128)(2,1)S(1)}, bf16[272,1280]{1,0:T(8,128)(2,1)S(1)}, u32[]{:S(2)}, u32[]{:S(2)}) collective-permute-start(bf16[272,1280]{1,0:T(8,128)(2,1)S(1)} %get-tuple-element.67), channel_id=1, source_target_pairs={{0,192},{1,193},{2,194},{3,195},{4,196},{5,197},{6,198},{7,199},{8... | collective-permute-start | bytes 2088968 | tf_op jit(solution)/shard_map/ppermute | solution.py:44
  89.8 11.4 %collective-permute-start.34 = (bf16[272,1280]{1,0:T(8,128)(2,1)S(1)}, bf16[272,1280]{1,0:T(8,128)(2,1)S(1)}, u32[]{:S(2)}, u32[]{:S(2)}) collective-permute-start(bf16[272,1280]{1,0:T(8,128)(2,1)S(1)} %get-tuple-element.65), channel_id=1, source_target_pairs={{0,64},{1,65},{2,66},{3,67},{4,68},{5,69},{6,70},{7,71},{8,72},{9,... | collective-permute-start | bytes 2088968 | tf_op jit(solution)/shard_map/ppermute | solution.py:44
  94.2 7.9 %collective-permute-start.32 = (bf16[144,1280]{1,0:T(8,128)(2,1)S(1)}, bf16[144,1280]{1,0:T(8,128)(2,1)S(1)}, u32[]{:S(2)}, u32[]{:S(2)}) collective-permute-start(bf16[144,1280]{1,0:T(8,128)(2,1)S(1)} %ring_fold.3), channel_id=1, source_target_pairs={{0,7},{1,0},{2,1},{3,2},{4,3},{5,4},{6,5},{7,6},{8,15},{9,8},{10,9... | collective-permute-start | bytes 1105928 | tf_op jit(solution)/shard_map/ppermute | solution.py:44
  102.3 5.9 %collective-permute-start.36 = (bf16[80,1280]{1,0:T(8,128)(2,1)S(1)}, bf16[80,1280]{1,0:T(8,128)(2,1)S(1)}, u32[]{:S(2)}, u32[]{:S(2)}) collective-permute-start(bf16[80,1280]{1,0:T(8,128)(2,1)S(1)} %get-tuple-element.71), channel_id=1, source_target_pairs={{0,7},{1,0},{2,1},{3,2},{4,3},{5,4},{6,5},{7,6},{8,15},{9,8},{10,9... | collective-permute-start | bytes 614408 | tf_op jit(solution)/shard_map/ppermute | solution.py:44
  103.1 9.5 %collective-permute-start.38 = (bf16[80,1280]{1,0:T(8,128)(2,1)S(1)}, bf16[80,1280]{1,0:T(8,128)(2,1)S(1)}, u32[]{:S(2)}, u32[]{:S(2)}) collective-permute-start(bf16[80,1280]{1,0:T(8,128)(2,1)S(1)} %get-tuple-element.72), channel_id=1, source_target_pairs={{0,40},{1,41},{2,42},{3,43},{4,44},{5,45},{6,46},{7,47},{8,0},{9,1... | collective-permute-start | bytes 614408 | tf_op jit(solution)/shard_map/ppermute | solution.py:44
  103.6 9.1 %collective-permute-start.39 = (bf16[80,1280]{1,0:T(8,128)(2,1)S(1)}, bf16[80,1280]{1,0:T(8,128)(2,1)S(1)}, u32[]{:S(2)}, u32[]{:S(2)}) collective-permute-start(bf16[80,1280]{1,0:T(8,128)(2,1)S(1)} %get-tuple-element.73), channel_id=1, source_target_pairs={{0,8},{1,9},{2,10},{3,11},{4,12},{5,13},{6,14},{7,15},{8,32},{9,33... | collective-permute-start | bytes 614408 | tf_op jit(solution)/shard_map/ppermute | solution.py:44
  104.6 8.1 %collective-permute-start.40 = (bf16[80,1280]{1,0:T(8,128)(2,1)S(1)}, bf16[80,1280]{1,0:T(8,128)(2,1)S(1)}, u32[]{:S(2)}, u32[]{:S(2)}) collective-permute-start(bf16[80,1280]{1,0:T(8,128)(2,1)S(1)} %get-tuple-element.74), channel_id=1, source_target_pairs={{0,32},{1,33},{2,34},{3,35},{4,36},{5,37},{6,38},{7,39},{8,40},{9,... | collective-permute-start | bytes 614408 | tf_op jit(solution)/shard_map/ppermute | solution.py:44
  108.2 10.0 %collective-permute-start.37 = (bf16[80,1280]{1,0:T(8,128)(2,1)S(1)}, bf16[80,1280]{1,0:T(8,128)(2,1)S(1)}, u32[]{:S(2)}, u32[]{:S(2)}) collective-permute-start(bf16[80,1280]{1,0:T(8,128)(2,1)S(1)} %collective-permute-done.36.refs_3_), channel_id=1, source_target_pairs={{0,16},{1,17},{2,18},{3,19},{4,20},{5,21},{6,22},{7,23},{8,24},{9,... | collective-permute-start | bytes 614408 | tf_op jit(solution)/shard_map/ppermute | solution.py:44
  112.6 5.5 %collective-permute-start.35 = (bf16[64,1280]{1,0:T(8,128)(2,1)S(1)}, bf16[64,1280]{1,0:T(8,128)(2,1)S(1)}, u32[]{:S(2)}, u32[]{:S(2)}) collective-permute-start(bf16[64,1280]{1,0:T(8,128)(2,1)S(1)} %get-tuple-element.70), channel_id=1, source_target_pairs={{0,7},{1,0},{2,1},{3,2},{4,3},{5,4},{6,5},{7,6},{8,15},{9,8},{10,9... | collective-permute-start | bytes 491528 | tf_op jit(solution)/shard_map/ppermute | solution.py:44
